TPU v7x, 256 devices: a whole 4x4x8 slice. The times are simulated.
256 devices in a mesh: row: 64 (over x, y_hi, z), chan: 4 (over y_lo, core).
Axes of the slice: x: 4, y: 4 (y_hi: 2, y_lo: 2; y = y_hi * 2 + y_lo), z: 8, core: 2. Of those that a mesh axis runs over, the one named last changes fastest.
Arguments:
- image: bfloat16 [32, 4096, 4096], P('chan', 'row'), may hold values from -6 to 6
- spec_weight: bfloat16 [2, 256, 32, 32, 256], P(None, 'row', None, 'chan'), may hold values from -0.75 to 0.75
- point_weight: bfloat16 [32, 32], replicated, may hold values from -1 to 1
- bias: float32 [32], P('chan'), may hold values from -3 to 3
Outputs:
- layer_out: bfloat16 [32, 4096, 4096], P('chan', 'row')
All inputs are finite; a program needn't handle non-finite values.
Results may differ from a plain program's by a relative error of at most 0.012.
Values may be sent and summed in bfloat16 or wider, within the bound.
No kernel may reach another device: no remote copies, remote signals or barrier semaphores. Data moves between devices by JAX's collectives and lax.ppermute only.
A program may use at most 128 MiB of HBM per device.

v0:
```python
import math

import jax
import jax.numpy as jnp
from jax import lax
from jax.sharding import PartitionSpec as P

H = 4096
W = 4096
MX = 256
MY = 256


def wave_table(points, freqs, length):
    prod = jnp.mod(points[:, None] * freqs[None, :], length)
    angle = prod.astype(jnp.float32) * (2.0 * math.pi / length)
    return (jnp.cos(angle), jnp.sin(angle))


def on_device(image, spec_weight, point_weight, bias):
    chan_count, row_count, width_len = image.shape
    row_index = lax.axis_index("row")
    row_devs = lax.axis_size("row")
    chan_index = lax.axis_index("chan")
    row_global = row_index * row_count + jnp.arange(row_count, dtype=jnp.int32)
    col_pts = jnp.arange(W, dtype=jnp.int32)
    col_freq = jnp.arange(MY, dtype=jnp.int32)
    cos_w, sin_w = wave_table(col_pts, col_freq, W)
    fwd_cols = jnp.concatenate([cos_w, -sin_w], 1).astype(jnp.bfloat16)
    back_cols = jnp.concatenate([cos_w.T, -sin_w.T], 0).astype(jnp.bfloat16)
    row_freq = jnp.arange(MX, dtype=jnp.int32) - MX // 2
    colspec = jnp.dot(
        image.reshape(chan_count * row_count, width_len),
        fwd_cols,
        preferred_element_type=jnp.float32,
    )
    colspec = (
        (colspec * (1.0 / math.sqrt(W))).astype(jnp.bfloat16).reshape(chan_count, row_count, 2 * MY)
    )
    block_len = MX // row_devs
    cos_h, sin_h = wave_table(row_global, row_freq, H)
    fwd_rows = jnp.concatenate([cos_h, sin_h], 1).astype(jnp.bfloat16)
    partial_value = jnp.einsum("chp,hq->cqp", colspec, fwd_rows, preferred_element_type=jnp.float32)
    spec_re = partial_value[:, :MX, :MY] + partial_value[:, MX:, MY:]
    spec_im = partial_value[:, :MX, MY:] - partial_value[:, MX:, :MY]
    partial_value = jnp.concatenate([spec_re, spec_im], -1) * (1.0 / math.sqrt(H))
    summed = lax.psum(partial_value, "row")
    block = lax.dynamic_slice_in_dim(summed, row_index * block_len, block_len, 1)
    spectrum = block.astype(jnp.bfloat16)
    all_inputs = lax.all_gather(spectrum, "chan", axis=0, tiled=True)
    zed_re = all_inputs[..., :MY].astype(jnp.float32)
    zed_im = all_inputs[..., MY:].astype(jnp.float32)
    wgt_re = spec_weight[0].astype(jnp.float32)
    wgt_im = spec_weight[1].astype(jnp.float32)
    mix_re = jnp.einsum("kiop,ikp->okp", wgt_re, zed_re) - jnp.einsum(
        "kiop,ikp->okp", wgt_im, zed_im
    )
    mix_im = jnp.einsum("kiop,ikp->okp", wgt_re, zed_im) + jnp.einsum(
        "kiop,ikp->okp", wgt_im, zed_re
    )
    mixed = jnp.concatenate([mix_re, mix_im], -1).astype(jnp.bfloat16)
    piece = lax.all_gather(mixed, "row", axis=1, tiled=True)
    freq_now = jnp.arange(piece.shape[1], dtype=jnp.int32) - MX // 2
    cos_back, sin_back = wave_table(freq_now, row_global, H)
    with_cos = jnp.einsum(
        "okp,kh->ohp", piece, cos_back.astype(jnp.bfloat16), preferred_element_type=jnp.float32
    )
    with_sin = jnp.einsum(
        "okp,kh->ohp", piece, sin_back.astype(jnp.bfloat16), preferred_element_type=jnp.float32
    )
    back_re = with_cos[..., :MY] - with_sin[..., MY:]
    back_im = with_sin[..., :MY] + with_cos[..., MY:]
    back_re, back_im = (back_re, back_im)
    rowback = (jnp.concatenate([back_re, back_im], -1) * (1.0 / math.sqrt(MX))).astype(jnp.bfloat16)
    spectral = jnp.dot(
        rowback.reshape(chan_count * row_count, 2 * MY),
        back_cols,
        preferred_element_type=jnp.float32,
    )
    spectral = (spectral * (1.0 / math.sqrt(MY))).reshape(chan_count, row_count, width_len)
    piece = lax.all_gather(image, "chan", axis=0, tiled=True)
    weight_cols = lax.dynamic_slice(
        point_weight, (chan_index * chan_count, 0), (chan_count, piece.shape[0])
    )
    pointwise = jnp.einsum(
        "oi,ihw->ohw", weight_cols, piece, preferred_element_type=jnp.float32
    ).astype(jnp.bfloat16)
    total = spectral + pointwise.astype(jnp.float32) + bias[:, None, None]
    return jax.nn.gelu(total, approximate=False).astype(jnp.bfloat16)


def solution(mesh):
    in_specs = (P("chan", "row", None), P(None, "row", None, "chan", None), P(), P("chan"))
    out_specs = P("chan", "row", None)
    return jax.shard_map(
        on_device, mesh=mesh, in_specs=in_specs, out_specs=out_specs, check_vma=False
    )
```

profile of v0, /device:TPU:32, one launch (start us, length us, event | category | flops | bytes accessed | tf_op | source)
XLA Modules:
  0.0 765.2 jit_solution(13767197899245018390)
XLA Ops:
  6.5 0.0 copy-start
  6.5 0.0 all-gather.3.cloned.1.call-start
  6.5 17.8 %negate_convert_fusion.1 = (bf16[4096,256]{1,0:T(8,128)(2,1)S(1)}, bf16[4096,256]{1,0:T(8,128)(2,1)}) fusion(), kind=kLoop, calls=%fused_computation.47 | loop fusion | flops 17825792 | bytes 4194304 | tf_op jit(solution)/shard_map/convert.7
  24.4 0.3 cosine_convert_fusion.2
  24.7 5.2 fusion.43
  30.0 4.5 fusion.61
  34.5 10.4 %copy.14 = f32[512,8,512]{2,1,0:T(8,128)} copy(f32[512,8,512]{0,2,1:T(8,128)} %fusion.61) | data formatting | bytes 16777216 | tf_op jit(solution)/shard_map/chp,hq->cqp/dot_general | solution.py:43
  44.9 4.0 slice_add_fusion
  48.9 0.0 copy-start.2
  48.9 2.7 maximum_multiply_fusion
  51.6 403.4 %all-reduce.1 = bf16[8,256,512]{2,0,1:T(8,128)(2,1)S(1)} all-reduce(f32[8,256,512]{2,0,1:T(8,128)} %maximum_multiply_fusion), channel_id=1, replica_groups=mesh['row'=64,'chan'=4] {'row'}, use_global_device_ids=true, to_apply=%region_0.1 | all-reduce | flops 1048576 | bytes 6291456 | tf_op jit(solution)/shard_map/psum | solution.py:47
  455.1 5.4 all_gather.9
  460.6 0.0 copy-done.2
  460.6 0.3 fusion.48
  461.0 0.6 pad_maximum_fusion
  461.6 0.0 all-gather.3.cloned.1.call-update
  461.6 0.0 all-gather.5.cloned.1.call-start
  461.7 6.5 copy.18
  468.2 0.0 all-gather.5.cloned.1.call-update
  468.2 17.8 %negate_convert_fusion = (bf16[256,4096]{1,0:T(8,128)(2,1)S(1)}, bf16[256,4096]{1,0:T(8,128)(2,1)}) fusion(), kind=kLoop, calls=%fused_computation.43 | loop fusion | flops 17825792 | bytes 4194304 | tf_op jit(solution)/shard_map/convert.1
  486.0 92.3 %all-gather.3.cloned.1.call-done = bf16[8,256,512]{2,0,1:T(8,128)(2,1)} async-done(((bf16[8,4,512]{2,0,1:T(8,128)(2,1)}), bf16[8,256,512]{2,0,1:T(8,128)(2,1)}) %all-gather.3.cloned.1.call-update) | async-done | bytes 2097168 | tf_op jit(solution)/shard_map/all_gather | solution.py:62
  578.3 3.3 fusion.37
  581.7 3.2 fusion.40
  584.9 0.1 slice_subtract_fusion.1
  585.1 0.0 copy-done.1
  585.1 0.0 copy-start.3
  585.1 6.5 convolution_multiply_fusion
  591.6 137.9 %all-gather.5.cloned.1.call-done = bf16[32,64,4096]{2,0,1:T(8,128)(2,1)} async-done(((bf16[8,64,4096]{2,0,1:T(8,128)(2,1)}), bf16[32,64,4096]{2,0,1:T(8,128)(2,1)}) %all-gather.5.cloned.1.call-update) | async-done | bytes 16777232 | tf_op jit(solution)/shard_map/all_gather | solution.py:81
  729.5 0.0 copy-done
  729.5 0.0 copy-done.3
  729.5 24.5 %fusion.2 = bf16[8,64,4096]{2,0,1:T(8,128)(2,1)S(1)} fusion(f32[8,64,4096]{2,1,0:T(8,128)} %bitcast.62, f32[8]{0:T(128)S(1)} %copy-done.3, bf16[32,64,4096]{2,0,1:T(8,128)(2,1)} %all-gather.5.cloned.1.call-done, bf16[32,32]{1,0:T(8,128)(2,1)S(1)} %copy-done, s32[]{:T(128)S(6)} %select_n.38), kind=kOutput, calls=%fused_computation.3 | convolution fusion | flops 278921216 | bytes 29362692 | tf_op jit(solution)/shard_map/oi,ihw->ohw/dot_general | solution.py:85
  754.0 4.3 copy.20
  (10 shorter events, 0.1 us)
Async XLA Ops:
  6.5 722.9 %copy-start = (bf16[32,32]{1,0:T(8,128)(2,1)S(1)}, bf16[32,32]{1,0:T(8,128)(2,1)}, u32[]{:S(2)}) copy-start(bf16[32,32]{1,0:T(8,128)(2,1)} %param.6) | copy-start | bytes 6148
  6.5 571.8 %all-gather.3.cloned.1.call-start = ((), (), s32[]{:S(2)}) async-start(), calls=%async_computation | async-start | bytes 2129920 | tf_op jit(solution)/shard_map/all_gather | solution.py:62
  48.9 411.7 %copy-start.2 = (bf16[2,4,32,8,256]{4,3,2,1,0:T(8,128)(2,1)S(1)}, bf16[2,4,32,8,256]{4,3,2,1,0:T(8,128)(2,1)}, u32[]{:S(2)}) copy-start(bf16[2,4,32,8,256]{4,3,2,1,0:T(8,128)(2,1)} %param.5) | copy-start | bytes 3145732
  461.6 267.8 %all-gather.5.cloned.1.call-start = ((), (), s32[]{:S(2)}) async-start(), calls=%async_computation.1 | async-start | bytes 20971520 | tf_op jit(solution)/shard_map/all_gather | solution.py:81
  578.3 6.7 copy-start.1
  585.1 144.4 %copy-start.3 = (f32[8]{0:T(128)S(1)}, f32[8]{0:T(128)}, u32[]{:S(2)}) copy-start(f32[8]{0:T(128)} %param.7) | copy-start | bytes 100
Sparse Core Ops, SparseCore 0:
  461.8 116.5 all-gather.2
  580.1 149.2 all-gather.4
where the time goes:
time: 769 us; the launch traced here: 765 us
  blocking collectives  409 us (53%)
  waiting for transfers between devices  230 us (30%)
  matrix products  47.4 us (6%)
  other arithmetic  43.8 us (6%)
  local copies, waits for them, and re-layouts  21.3 us (3%)
  between operations  13.6 us (2%)
    psum x1, blocking collectives, on_device(): summed = lax.psum(partial_value, 'row')  403 us
    all_gather x1, waiting for transfers between devices, on_device(): piece = lax.all_gather(image, 'chan', axis=0, tiled=True)  138 us
    all_gather x1, waiting for transfers between devices, on_device(): piece = lax.all_gather(mixed, 'row', axis=1, tiled=True)  92.3 us
    another operation x3, other arithmetic  36 us
    dot_general x1, matrix products, on_device(): jnp.einsum('oi,ihw->ohw', weight_cols, piece, preferred_element_type=jnp....  24.5 us
  transfers between devices with their start and end apart: 2, of which 2 were waited for; matrix products, arithmetic and copies ran while one was open for 5% of the time, Pallas kernels for 0%

commit v1 on v0

v1 whole, which is shorter than its diff:
```python
import math

import jax
import jax.numpy as jnp
import ml_dtypes
import numpy as np
from jax import lax
from jax.sharding import Mesh, PartitionSpec as P

H = 4096
W = 4096
MX = 256
MY = 256
PAIR = [(0, 1), (1, 0)]
CHUNKS = 4


def wave_table(points, freqs, length):
    prod = np.mod(points[:, None] * freqs[None, :], length)
    one = np.arange(length).astype(np.float32) * np.float32(2.0 * math.pi / length)
    return np.cos(one)[prod], np.sin(one)[prod]


def tables():
    cos_w, sin_w = wave_table(np.arange(W), np.arange(MY), W)
    cols = np.concatenate([cos_w, -sin_w], 1)
    cos_h, sin_h = wave_table(np.arange(H), np.arange(MX) - MX // 2, H)
    rows = np.concatenate([cos_h, sin_h], 1)
    return cols.astype(ml_dtypes.bfloat16), rows.astype(ml_dtypes.bfloat16)


def on_device(image, spec_weight, point_weight, bias):
    chan, rows, width = image.shape
    cols_np, rows_np = tables()
    fwd_cols = jnp.asarray(cols_np)
    back_cols = jnp.asarray(np.ascontiguousarray(cols_np.T))
    row_group = lax.axis_index(("x", "yh")) * (8 * rows)
    row_tab = lax.dynamic_slice_in_dim(jnp.asarray(rows_np), row_group, 8 * rows, 0)

    step = rows // CHUNKS
    sibling = lax.ppermute(image, "core", PAIR)
    cross = [lax.ppermute(image[:, j * step : (j + 1) * step], "yl", PAIR) for j in range(CHUNKS)]
    cross_sib = [lax.ppermute(c, "core", PAIR) for c in cross]

    with jax.named_scope("colspec"):
        colspec = jnp.dot(
            image.reshape(chan * rows, width), fwd_cols, preferred_element_type=jnp.float32
        )
        colspec = (colspec * (1.0 / math.sqrt(W))).astype(jnp.bfloat16)
    with jax.named_scope("swap_rows"):
        line = lax.all_to_all(colspec.reshape(chan, rows, 2 * MY), "z", 0, 0, tiled=True)
    line = line.reshape(8 * rows, 2 * MY)
    with jax.named_scope("row_dft"):
        part = lax.dot_general(
            row_tab, line, (((0,), (0,)), ((), ())), preferred_element_type=jnp.float32
        )
        spec_re = part[:MX, :MY] + part[MX:, MY:]
        spec_im = part[:MX, MY:] - part[MX:, :MY]
        part = jnp.concatenate([spec_re, spec_im], -1) * (1.0 / math.sqrt(H))
        part = part.astype(jnp.bfloat16).reshape(64, MX // 64, 2 * MY)
    with jax.named_scope("swap_modes"):
        part = lax.all_to_all(part, ("x", "yh", "z"), 0, 0, tiled=True)
    with jax.named_scope("sum_lines"):
        spectrum = jnp.sum(
            part.reshape(8, 8, MX // 64, 2 * MY).astype(jnp.float32), 0
        ).astype(jnp.bfloat16)
    with jax.named_scope("gather_chan"):
        zed = lax.all_gather(spectrum, ("yl", "core"), axis=0, tiled=True)
    with jax.named_scope("mix"):
        zed_re = zed[..., :MY].astype(jnp.float32)
        zed_im = zed[..., MY:].astype(jnp.float32)
        wgt_re = spec_weight[0].astype(jnp.float32)
        wgt_im = spec_weight[1].astype(jnp.float32)
        mix_re = jnp.einsum("kiop,ikp->okp", wgt_re, zed_re) - jnp.einsum(
            "kiop,ikp->okp", wgt_im, zed_im
        )
        mix_im = jnp.einsum("kiop,ikp->okp", wgt_re, zed_im) + jnp.einsum(
            "kiop,ikp->okp", wgt_im, zed_re
        )
        mixed = jnp.concatenate([mix_re, mix_im], -1).astype(jnp.bfloat16)
        mixed = jnp.broadcast_to(mixed[None], (8,) + mixed.shape).reshape(64, MX // 64, 2 * MY)
    with jax.named_scope("spread_modes"):
        modes = lax.all_to_all(mixed, ("x", "yh", "z"), 0, 0, tiled=True).reshape(MX, 2 * MY)
    with jax.named_scope("rowback"):
        mode_re, mode_im = modes[:, :MY], modes[:, MY:]
        turned = jnp.concatenate(
            [modes, jnp.concatenate([-mode_im, mode_re], 1)], 0
        )
        back = jnp.dot(row_tab, turned, preferred_element_type=jnp.float32)
        back = (back * (1.0 / math.sqrt(MX))).astype(jnp.bfloat16).reshape(8, rows, 2 * MY)
    with jax.named_scope("swap_back"):
        back = lax.all_to_all(back, "z", 0, 0, tiled=True)
    with jax.named_scope("final"):
        spectral = jnp.dot(
            back.reshape(chan * rows, 2 * MY), back_cols, preferred_element_type=jnp.float32
        )
        spectral = (spectral * (1.0 / math.sqrt(MY))).reshape(chan, rows, width)
        me = lax.axis_index(("yl", "core"))
        mine = lax.dynamic_slice(point_weight, (me * chan, 0), (chan, 4 * chan))
        blocks = [
            lax.dynamic_slice(mine, (0, (me ^ s) * chan), (chan, chan)) for s in range(4)
        ]
        order = jnp.concatenate(blocks, 1)
        feats = jnp.concatenate(
            [image, sibling, jnp.concatenate(cross, 1), jnp.concatenate(cross_sib, 1)], 0
        )
        pointwise = jnp.einsum(
            "oi,ihw->ohw", order, feats, preferred_element_type=jnp.float32
        ).astype(jnp.bfloat16)
        total = spectral + pointwise.astype(jnp.float32) + bias[:, None, None]
        return jax.nn.gelu(total, approximate=False).astype(jnp.bfloat16)


def solution(mesh):
    fine = Mesh(mesh.devices.reshape(4, 2, 8, 2, 2), ("x", "yh", "z", "yl", "core"))
    row, chan = ("x", "yh", "z"), ("yl", "core")
    in_specs = (P(chan, row, None), P(None, row, None, chan, None), P(), P(chan))
    return jax.shard_map(
        on_device, mesh=fine, in_specs=in_specs, out_specs=P(chan, row, None), check_vma=False
    )
```

time: 769 us -> 207 us (0.27)
  blocking collectives: 409 us -> 5.43 us
  waiting for transfers between devices: 230 us -> 107 us
  other arithmetic: 43.8 us -> 1.42 us
  starting transfers between devices: 0.04 us -> 33.2 us
  between operations: 13.6 us -> 0.2 us
    psum x1 -> x0, blocking collectives: 403 us -> none  [on_device(): summed = lax.psum(partial_value, 'row')]
    all_gather x2 -> x0, waiting for transfers between devices: 230 us -> none  [the longest x1 138 us: on_device(): piece = lax.all_gather(image, 'chan', axis=0, tiled=True)]
    ppermute x0 -> x9, waiting for transfers between devices: none -> 76.1 us  [the longest x4 76.1 us: on_device(): lax.ppermute(image[:, j * step:(j + 1) * step], 'yl', PAIR)]
    another operation x3 -> x0, other arithmetic: 36 us -> none
    all_to_all x0 -> x4, waiting for transfers between devices: none -> 31.3 us  [the longest x1 16 us: on_device(): lax.all_to_all(colspec.reshape(chan, rows, 2 * MY), 'z', 0, 0, tiled=True)]
    all_to_all x0 -> x4, starting transfers between devices: none -> 29.2 us  [the longest x1 8.95 us: on_device(): part = lax.all_to_all(part, ('x', 'yh', 'z'), 0, 0, tiled=True)]
    dot_general x1 -> x0, local copies, waits for them, and re-layouts: 10.4 us -> none  [on_device(): jnp.einsum('chp,hq->cqp', colspec, fwd_rows, preferred_element_type=jnp.f...]
    dot_general x6 -> x5, matrix products: 47.4 us -> 40.9 us  [the longest x1 25.9 us: on_device(): jnp.einsum('oi,ihw->ohw', order, feats, preferred_element_type=jnp.float32)]
  transfers between devices with their start and end apart: 2 -> 13, of which waited for: 2 -> 7; matrix products, arithmetic and copies ran while one was open for 5% -> 9% of each run, Pallas kernels for 0% -> 0%
where the time goes in v1:
time: 207 us; the launch traced here: 204 us
  waiting for transfers between devices  107 us (52%)
  matrix products  40.9 us (20%)
  starting transfers between devices  33.2 us (16%)
  local copies, waits for them, and re-layouts  15.9 us (8%)
  blocking collectives  5.43 us (3%)
    ppermute x4, waiting for transfers between devices, on_device(): lax.ppermute(image[:, j * step:(j + 1) * step], 'yl', PAIR)  76.1 us
    dot_general x1, matrix products, on_device(): jnp.einsum('oi,ihw->ohw', order, feats, preferred_element_type=jnp.float32)  25.9 us
    all_to_all x1, waiting for transfers between devices, on_device(): lax.all_to_all(colspec.reshape(chan, rows, 2 * MY), 'z', 0, 0, tiled=True)  16 us
    all_to_all x1, starting transfers between devices, on_device(): part = lax.all_to_all(part, ('x', 'yh', 'z'), 0, 0, tiled=True)  8.95 us
    all_to_all x1, starting transfers between devices, on_device(): lax.all_to_all(colspec.reshape(chan, rows, 2 * MY), 'z', 0, 0, tiled=True)  8.7 us
    all_to_all x1, waiting for transfers between devices, on_device(): part = lax.all_to_all(part, ('x', 'yh', 'z'), 0, 0, tiled=True)  8.18 us
    all_to_all x1, waiting for transfers between devices, on_device(): lax.all_to_all(mixed, ('x', 'yh', 'z'), 0, 0, tiled=True)  7.11 us
    all_to_all x1, starting transfers between devices, on_device(): lax.all_to_all(mixed, ('x', 'yh', 'z'), 0, 0, tiled=True)  7.07 us
  transfers between devices with their start and end apart: 13, of which 7 were waited for; matrix products, arithmetic and copies ran while one was open for 9% of the time, Pallas kernels for 0%

profile of v1, /device:TPU:32, one launch (start us, length us, event | category | flops | bytes accessed | tf_op | source)
XLA Modules:
  0.0 204.4 jit_solution(10309029177857765415)
XLA Ops:
  0.0 6.6 %fusion.34 = bf16[512,512]{0,1:T(8,128)(2,1)} fusion(bf16[512,4096]{1,0:T(8,128)(2,1)} %bitcast.52, bf16[4096,512]{1,0:T(8,128)(2,1)} %constant.148.clone), kind=kOutput, calls=%fused_computation.49 | convolution fusion | flops 2148007936 | bytes 8912896 | tf_op jit(solution)/shard_map/colspec/dot_general | solution.py:46
  6.6 8.7 %all-to-all-start = ((bf16[8,64,512]{2,1,0:T(8,128)(2,1)}), bf16[8,64,512]{2,1,0:T(8,128)(2,1)S(1)}, u32[]{:S(2)}, u32[]{:S(2)}) async-start(bf16[8,64,512]{2,1,0:T(8,128)(2,1)} %bitcast.10), calls=%async_computation | async-start | bytes 1048576 | tf_op jit(solution)/shard_map/swap_rows/all_to_all | solution.py:51
  15.3 16.0 %all-to-all-done = bf16[8,64,512]{2,1,0:T(8,128)(2,1)S(1)} async-done(((bf16[8,64,512]{2,1,0:T(8,128)(2,1)}), bf16[8,64,512]{2,1,0:T(8,128)(2,1)S(1)}, u32[]{:S(2)}, u32[]{:S(2)}) %all-to-all-start) | async-done | bytes 524320 | tf_op jit(solution)/shard_map/swap_rows/all_to_all | solution.py:51
  31.3 1.5 fusion.41
  32.8 0.1 slice_add_fusion
  32.9 0.1 concatenate.34
  33.0 0.1 concatenate.35
  33.1 0.8 fusion.43
  33.9 9.0 %all-to-all-start.1 = ((bf16[64,4,512]{2,1,0:T(4,128)(2,1)}), bf16[64,4,512]{2,1,0:T(4,128)(2,1)S(1)}, u32[]{:S(2)}, u32[]{:S(2)}) async-start(bf16[64,4,512]{2,1,0:T(4,128)(2,1)} %fusion.43), calls=%async_computation.1 | async-start | bytes 524288 | tf_op jit(solution)/shard_map/swap_modes/all_to_all | solution.py:62
  42.9 6.5 %copy.23 = bf16[8,64,4096]{2,0,1:T(8,128)(2,1)} copy(bf16[8,64,4096]{2,1,0:T(8,128)(2,1)} %param.7) | data formatting | bytes 8388608 | tf_op args[0]
  49.4 8.2 %all-to-all-done.1 = bf16[64,4,512]{2,1,0:T(4,128)(2,1)S(1)} async-done(((bf16[64,4,512]{2,1,0:T(4,128)(2,1)}), bf16[64,4,512]{2,1,0:T(4,128)(2,1)S(1)}, u32[]{:S(2)}, u32[]{:S(2)}) %all-to-all-start.1) | async-done | bytes 262176 | tf_op jit(solution)/shard_map/swap_modes/all_to_all | solution.py:62
  57.6 0.1 reduce_sum.12
  57.7 5.4 %all_gather.3 = bf16[32,4,512]{2,1,0:T(4,128)(2,1)S(1)} all-gather(bf16[8,4,512]{2,1,0:T(4,128)(2,1)S(1)} %reduce_sum.12), channel_id=1, replica_groups=mesh['x'=4,'yh'=2,'z'=8,'yl'=2,'core'=2] {'yl','core'}, dimensions={0}, use_global_device_ids=true | all-gather | bytes 163840 | tf_op jit(solution)/shard_map/gather_chan/all_gather | solution.py:68
  63.2 0.3 fusion.38
  63.6 0.8 broadcast_in_dim.2
  64.4 7.1 %all-to-all-start.2 = ((bf16[64,4,512]{2,1,0:T(4,128)(2,1)}), bf16[64,4,512]{2,1,0:T(4,128)(2,1)S(1)}, u32[]{:S(2)}, u32[]{:S(2)}) async-start(bf16[64,4,512]{2,1,0:T(4,128)(2,1)} %bitcast.21), calls=%async_computation.2 | async-start | bytes 524288 | tf_op jit(solution)/shard_map/spread_modes/all_to_all | solution.py:83
  71.5 3.9 %fusion.65 = (bf16[8,16,4096]{2,0,1:T(8,128)(2,1)}, bf16[8,16,4096]{2,0,1:T(8,128)(2,1)}, bf16[8,16,4096]{2,0,1:T(8,128)(2,1)S(1)}, bf16[8,16,4096]{2,0,1:T(8,128)(2,1)S(1)}) fusion(bf16[8,64,4096]{2,0,1:T(8,128)(2,1)} %copy.23), kind=kLoop, calls=%fused_computation.88 | loop fusion | bytes 8388608 | tf_op jit(solution)/shard_map/slice | solution.py:42
  75.4 0.7 collective-permute-start.1
  76.1 1.3 collective-permute-start.4
  77.4 0.7 collective-permute-start.3
  78.1 1.3 collective-permute-start.2
  79.5 7.1 %all-to-all-done.2 = bf16[64,4,512]{2,1,0:T(4,128)(2,1)S(1)} async-done(((bf16[64,4,512]{2,1,0:T(4,128)(2,1)}), bf16[64,4,512]{2,1,0:T(4,128)(2,1)S(1)}, u32[]{:S(2)}, u32[]{:S(2)}) %all-to-all-start.2) | async-done | bytes 262176 | tf_op jit(solution)/shard_map/spread_modes/all_to_all | solution.py:83
  86.7 2.3 %fusion.35 = bf16[512,512]{1,0:T(8,128)(2,1)} fusion(bf16[4096,512]{1,0:T(8,128)(2,1)} %constant.150.clone, s32[]{:T(128)S(6)} %select_n.24, bf16[256,256]{1,0:T(8,128)(2,1)S(1)} %get-tuple-element.18, bf16[256,256]{1,0:T(8,128)(2,1)S(1)} %get-tuple-element.17, bf16[256,512]{1,0:T(8,128)(2,1)S(1)} %reshape.51), kind=kOutput, calls=%fused_computation.50 | convolution fusion | flops 270532608 | bytes 1572868 | tf_op jit(solution)/shard_map/rowback/dot_general | solution.py:89
  89.0 4.4 %all-to-all-start.3 = ((bf16[8,64,512]{2,1,0:T(8,128)(2,1)}), bf16[8,64,512]{2,1,0:T(8,128)(2,1)S(1)}, u32[]{:S(2)}, u32[]{:S(2)}) async-start(bf16[8,64,512]{2,1,0:T(8,128)(2,1)} %bitcast.22), calls=%async_computation.3 | async-start | bytes 1048576 | tf_op jit(solution)/shard_map/swap_back/all_to_all | solution.py:92
  93.4 9.4 %collective-permute-done.1 = bf16[8,16,4096]{2,0,1:T(8,128)(2,1)} collective-permute-done((bf16[8,16,4096]{2,0,1:T(8,128)(2,1)}, bf16[8,16,4096]{2,0,1:T(8,128)(2,1)}, u32[]{:S(2)}, u32[]{:S(2)}) %collective-permute-start.1) | collective-permute-done | bytes 1048608 | tf_op jit(solution)/shard_map/ppermute | solution.py:42
  102.8 22.5 %collective-permute-done.4 = bf16[8,16,4096]{2,0,1:T(8,128)(2,1)} collective-permute-done((bf16[8,16,4096]{2,0,1:T(8,128)(2,1)}, bf16[8,16,4096]{2,0,1:T(8,128)(2,1)}, u32[]{:S(2)}, u32[]{:S(2)}) %collective-permute-start.4) | collective-permute-done | bytes 1048608 | tf_op jit(solution)/shard_map/ppermute | solution.py:42
  125.3 22.5 %collective-permute-done.3 = bf16[8,16,4096]{2,0,1:T(8,128)(2,1)} collective-permute-done((bf16[8,16,4096]{2,0,1:T(8,128)(2,1)S(1)}, bf16[8,16,4096]{2,0,1:T(8,128)(2,1)}, u32[]{:S(2)}, u32[]{:S(2)}) %collective-permute-start.3) | collective-permute-done | bytes 1048608 | tf_op jit(solution)/shard_map/ppermute | solution.py:42
  147.8 21.7 %collective-permute-done.2 = bf16[8,16,4096]{2,0,1:T(8,128)(2,1)} collective-permute-done((bf16[8,16,4096]{2,0,1:T(8,128)(2,1)S(1)}, bf16[8,16,4096]{2,0,1:T(8,128)(2,1)}, u32[]{:S(2)}, u32[]{:S(2)}) %collective-permute-start.2) | collective-permute-done | bytes 1048608 | tf_op jit(solution)/shard_map/ppermute | solution.py:42
  169.5 0.1 fusion.66
  169.6 4.5 %convolution_multiply_fusion = f32[512,4096]{1,0:T(8,128)S(1)} fusion(bf16[512,512]{1,0:T(8,128)(2,1)S(1)} %bitcast.53, bf16[512,4096]{1,0:T(8,128)(2,1)} %constant.149.clone), kind=kOutput, calls=%fused_computation.41 | convolution fusion | flops 2149580800 | bytes 13107200 | tf_op jit(solution)/shard_map/final/dot_general | solution.py:94
  174.2 25.9 %fusion.22 = bf16[8,64,4096]{2,0,1:T(8,128)(2,1)S(1)} fusion(f32[8,64,4096]{2,1,0:T(8,128)S(1)} %bitcast.51, f32[8]{0:T(128)S(1)} %copy-done.2, bf16[8,16,4096]{2,0,1:T(8,128)(2,1)} %collective-permute-done.8, bf16[8,16,4096]{2,0,1:T(8,128)(2,1)S(1)} %collective-permute-done.7, bf16[8,16,4096]{2,0,1:T(8,128)(2,1)} %collective-permute-done.6, ...), kind=kOutput, calls=%fused_computation.23 | convolution fusion | flops 446695424 | bytes 29360672 | tf_op jit(solution)/shard_map/final/oi,ihw->ohw/dot_general | solution.py:107
  200.1 4.3 %copy.25 = bf16[8,64,4096]{2,1,0:T(8,128)(2,1)} copy(bf16[8,64,4096]{2,0,1:T(8,128)(2,1)S(1)} %fusion.22) | data formatting | bytes 8388608 | tf_op jit(solution)/shard_map/final/convert_element_type | solution.py:111
  (25 shorter events, 0.2 us)
Async XLA Ops:
  6.6 56.6 %copy-start = (bf16[2,4,32,8,256]{4,3,2,1,0:T(8,128)(2,1)S(1)}, bf16[2,4,32,8,256]{4,3,2,1,0:T(8,128)(2,1)}, u32[]{:S(2)}) copy-start(bf16[2,4,32,8,256]{4,3,2,1,0:T(8,128)(2,1)} %param.8) | copy-start | bytes 3145732
  6.6 24.7 %all-to-all-start = ((bf16[8,64,512]{2,1,0:T(8,128)(2,1)}), bf16[8,64,512]{2,1,0:T(8,128)(2,1)S(1)}, u32[]{:S(2)}, u32[]{:S(2)}) async-start(bf16[8,64,512]{2,1,0:T(8,128)(2,1)} %bitcast.10), calls=%async_computation | async-start | bytes 1048576 | tf_op jit(solution)/shard_map/swap_rows/all_to_all | solution.py:51
  33.9 23.6 %all-to-all-start.1 = ((bf16[64,4,512]{2,1,0:T(4,128)(2,1)}), bf16[64,4,512]{2,1,0:T(4,128)(2,1)S(1)}, u32[]{:S(2)}, u32[]{:S(2)}) async-start(bf16[64,4,512]{2,1,0:T(4,128)(2,1)} %fusion.43), calls=%async_computation.1 | async-start | bytes 524288 | tf_op jit(solution)/shard_map/swap_modes/all_to_all | solution.py:62
  49.4 124.8 %collective-permute-start = (bf16[8,64,4096]{2,0,1:T(8,128)(2,1)}, bf16[8,64,4096]{2,0,1:T(8,128)(2,1)}, u32[]{:S(2)}, u32[]{:S(2)}) collective-permute-start(bf16[8,64,4096]{2,0,1:T(8,128)(2,1)} %copy.23), channel_id=1, source_target_pairs={{0,1},{1,0},{2,3},{3,2},{4,5},{5,4},{6,7},{7,6},{8,9},{9,8},{10,11... | collective-permute-start | bytes 12582920 | tf_op jit(solution)/shard_map/ppermute | solution.py:41
  63.1 106.4 %copy-start.1 = (bf16[32,32]{1,0:T(8,128)(2,1)S(1)}, bf16[32,32]{1,0:T(8,128)(2,1)}, u32[]{:S(2)}) copy-start(bf16[32,32]{1,0:T(8,128)(2,1)} %param.9) | copy-start | bytes 6148
  64.4 22.2 %all-to-all-start.2 = ((bf16[64,4,512]{2,1,0:T(4,128)(2,1)}), bf16[64,4,512]{2,1,0:T(4,128)(2,1)S(1)}, u32[]{:S(2)}, u32[]{:S(2)}) async-start(bf16[64,4,512]{2,1,0:T(4,128)(2,1)} %bitcast.21), calls=%async_computation.2 | async-start | bytes 524288 | tf_op jit(solution)/shard_map/spread_modes/all_to_all | solution.py:83
  75.4 27.4 %collective-permute-start.1 = (bf16[8,16,4096]{2,0,1:T(8,128)(2,1)}, bf16[8,16,4096]{2,0,1:T(8,128)(2,1)}, u32[]{:S(2)}, u32[]{:S(2)}) collective-permute-start(bf16[8,16,4096]{2,0,1:T(8,128)(2,1)} %get-tuple-element.11), channel_id=1, source_target_pairs={{0,2},{2,0},{1,3},{3,1},{4,6},{6,4},{5,7},{7,5},{8,10},{10,8},{9,1... | collective-permute-start | bytes 3145736 | tf_op jit(solution)/shard_map/ppermute | solution.py:42
  76.1 49.2 %collective-permute-start.4 = (bf16[8,16,4096]{2,0,1:T(8,128)(2,1)}, bf16[8,16,4096]{2,0,1:T(8,128)(2,1)}, u32[]{:S(2)}, u32[]{:S(2)}) collective-permute-start(bf16[8,16,4096]{2,0,1:T(8,128)(2,1)} %get-tuple-element.12), channel_id=1, source_target_pairs={{0,2},{2,0},{1,3},{3,1},{4,6},{6,4},{5,7},{7,5},{8,10},{10,8},{9,1... | collective-permute-start | bytes 3145736 | tf_op jit(solution)/shard_map/ppermute | solution.py:42
  77.4 70.3 %collective-permute-start.3 = (bf16[8,16,4096]{2,0,1:T(8,128)(2,1)S(1)}, bf16[8,16,4096]{2,0,1:T(8,128)(2,1)}, u32[]{:S(2)}, u32[]{:S(2)}) collective-permute-start(bf16[8,16,4096]{2,0,1:T(8,128)(2,1)S(1)} %get-tuple-element.13), channel_id=1, source_target_pairs={{0,2},{2,0},{1,3},{3,1},{4,6},{6,4},{5,7},{7,5},{8,10},{10,8},{9,1... | collective-permute-start | bytes 3145736 | tf_op jit(solution)/shard_map/ppermute | solution.py:42
  78.1 91.4 %collective-permute-start.2 = (bf16[8,16,4096]{2,0,1:T(8,128)(2,1)S(1)}, bf16[8,16,4096]{2,0,1:T(8,128)(2,1)}, u32[]{:S(2)}, u32[]{:S(2)}) collective-permute-start(bf16[8,16,4096]{2,0,1:T(8,128)(2,1)S(1)} %get-tuple-element.14), channel_id=1, source_target_pairs={{0,2},{2,0},{1,3},{3,1},{4,6},{6,4},{5,7},{7,5},{8,10},{10,8},{9,1... | collective-permute-start | bytes 3145736 | tf_op jit(solution)/shard_map/ppermute | solution.py:42
  86.7 87.5 %copy-start.2 = (f32[8]{0:T(128)S(1)}, f32[8]{0:T(128)}, u32[]{:S(2)}) copy-start(f32[8]{0:T(128)} %param.10) | copy-start | bytes 100
  89.0 80.6 %all-to-all-start.3 = ((bf16[8,64,512]{2,1,0:T(8,128)(2,1)}), bf16[8,64,512]{2,1,0:T(8,128)(2,1)S(1)}, u32[]{:S(2)}, u32[]{:S(2)}) async-start(bf16[8,64,512]{2,1,0:T(8,128)(2,1)} %bitcast.22), calls=%async_computation.3 | async-start | bytes 1048576 | tf_op jit(solution)/shard_map/swap_back/all_to_all | solution.py:92
  102.8 71.3 %collective-permute-start.5 = (bf16[8,16,4096]{2,0,1:T(8,128)(2,1)}, bf16[8,16,4096]{2,0,1:T(8,128)(2,1)}, u32[]{:S(2)}, u32[]{:S(2)}) collective-permute-start(bf16[8,16,4096]{2,0,1:T(8,128)(2,1)} %collective-permute-done.1), channel_id=1, source_target_pairs={{0,1},{1,0},{2,3},{3,2},{4,5},{5,4},{6,7},{7,6},{8,9},{9,8},{10,11... | collective-permute-start | bytes 3145736 | tf_op jit(solution)/shard_map/ppermute | solution.py:43
  125.3 48.8 %collective-permute-start.8 = (bf16[8,16,4096]{2,0,1:T(8,128)(2,1)}, bf16[8,16,4096]{2,0,1:T(8,128)(2,1)}, u32[]{:S(2)}, u32[]{:S(2)}) collective-permute-start(bf16[8,16,4096]{2,0,1:T(8,128)(2,1)} %collective-permute-done.4), channel_id=1, source_target_pairs={{0,1},{1,0},{2,3},{3,2},{4,5},{5,4},{6,7},{7,6},{8,9},{9,8},{10,11... | collective-permute-start | bytes 3145736 | tf_op jit(solution)/shard_map/ppermute | solution.py:43
  147.8 26.4 %collective-permute-start.7 = (bf16[8,16,4096]{2,0,1:T(8,128)(2,1)}, bf16[8,16,4096]{2,0,1:T(8,128)(2,1)S(1)}, u32[]{:S(2)}, u32[]{:S(2)}) collective-permute-start(bf16[8,16,4096]{2,0,1:T(8,128)(2,1)} %collective-permute-done.3), channel_id=1, source_target_pairs={{0,1},{1,0},{2,3},{3,2},{4,5},{5,4},{6,7},{7,6},{8,9},{9,8},{10,11... | collective-permute-start | bytes 3145736 | tf_op jit(solution)/shard_map/ppermute | solution.py:43
  169.5 4.7 %collective-permute-start.6 = (bf16[8,16,4096]{2,0,1:T(8,128)(2,1)}, bf16[8,16,4096]{2,0,1:T(8,128)(2,1)}, u32[]{:S(2)}, u32[]{:S(2)}) collective-permute-start(bf16[8,16,4096]{2,0,1:T(8,128)(2,1)} %collective-permute-done.2), channel_id=1, source_target_pairs={{0,1},{1,0},{2,3},{3,2},{4,5},{5,4},{6,7},{7,6},{8,9},{9,8},{10,11... | collective-permute-start | bytes 3145736 | tf_op jit(solution)/shard_map/ppermute | solution.py:43

commit v2 on v1

v2 whole, which is shorter than its diff:
```python
import functools
import math

import jax
import jax.numpy as jnp
import ml_dtypes
import numpy as np
from jax import lax
from jax.experimental import pallas as pl
from jax.experimental.pallas import tpu as pltpu
from jax.sharding import Mesh, PartitionSpec as P

H = 4096
W = 4096
MX = 256
MY = 256
PAIR = [(0, 1), (1, 0)]
GROUP = 16
VMEM = 56 * 2**20
TILE = 512
CUTS = (0, 1024, 2048, 3072, 4096)
RAW = 2


def wave_table(points, freqs, length):
    prod = np.mod(points[:, None] * freqs[None, :], length)
    one = np.arange(length).astype(np.float32) * np.float32(2.0 * math.pi / length)
    return np.cos(one)[prod], np.sin(one)[prod]


def tables():
    cos_w, sin_w = wave_table(np.arange(W), np.arange(MY), W)
    cols = np.concatenate([cos_w, -sin_w], 1)
    freq = np.arange(MX).reshape(4, 2, 8, 4).transpose(0, 2, 1, 3).reshape(-1) - MX // 2
    cos_h, sin_h = wave_table(np.arange(H), freq, H)
    rows = np.concatenate([cos_h, sin_h], 1).reshape(4, 8, 2 * 64, 2 * MX)
    return cols.astype(ml_dtypes.bfloat16), rows.astype(ml_dtypes.bfloat16)


def spread(point_weight, outputs, inputs, chan):
    mine = lax.dynamic_slice(point_weight, (outputs * chan, 0), (chan, 4 * chan))
    order = jnp.concatenate(
        [lax.dynamic_slice(mine, (0, i * chan), (chan, chan)) for i in inputs], 1
    )
    n = len(inputs) * chan
    tall = np.kron(np.eye(chan), np.ones((GROUP, 1)))
    wide = np.kron(np.eye(n), np.ones((1, GROUP)))
    same = np.tile(np.eye(GROUP), (chan, n))
    full = jnp.dot(jnp.asarray(tall, jnp.bfloat16), order)
    full = jnp.dot(full, jnp.asarray(wide, jnp.bfloat16))
    return full * jnp.asarray(same, jnp.bfloat16)


def product_kernel(own_ref, sib_ref, kron_ref, out_ref):
    for g in range(own_ref.shape[1] // GROUP):
        at = pl.ds(g * GROUP, GROUP)
        feats = jnp.concatenate(
            [r[:, at, :].reshape(8 * GROUP, TILE) for r in (own_ref, sib_ref)], 0
        )
        total = jnp.dot(kron_ref[...], feats, preferred_element_type=jnp.float32)
        out_ref[:, at, :] = total.astype(jnp.bfloat16).reshape(8, GROUP, TILE)


def product(begin, end, image, sibling, kron):
    chan, rows, _ = image.shape
    first, steps = begin // TILE, (end - begin) // TILE
    whole = pl.BlockSpec((chan, rows, TILE), lambda w: (0, 0, first + w))
    return pl.pallas_call(
        product_kernel,
        grid=(steps,),
        in_specs=[whole, whole, pl.BlockSpec(kron.shape, lambda w: (0, 0))],
        out_specs=pl.BlockSpec((chan, rows, TILE), lambda w: (0, 0, w)),
        out_shape=jax.ShapeDtypeStruct((chan, rows, end - begin), jnp.bfloat16),
        compiler_params=pltpu.CompilerParams(vmem_limit_bytes=VMEM),
        cost_estimate=pl.CostEstimate(
            flops=2 * 8 * rows * TILE * 256 * steps,
            bytes_accessed=3 * 2**19 * steps,
            transcendentals=0,
        ),
        name="product",
    )(image, sibling, kron)


def last_kernel(ends, raw, *refs):
    rb_ref, back_ref, own_ref, sib_ref, kron_ref, bias_ref = refs[:6]
    cross_refs, out_ref = refs[6:], refs[-1]
    rows = rb_ref.shape[1]

    def one(cross, is_raw):
        for g in range(rows // GROUP):
            at = pl.ds(g * GROUP, GROUP)
            feats = (own_ref, sib_ref, *cross) if is_raw else (own_ref, sib_ref)
            feats = jnp.concatenate([r[:, at, :].reshape(8 * GROUP, TILE) for r in feats], 0)
            total = jnp.dot(
                rb_ref[:, at, :].reshape(8 * GROUP, 2 * MY),
                back_ref[...],
                preferred_element_type=jnp.float32,
            )
            total += jnp.dot(
                kron_ref[:, : feats.shape[0]], feats, preferred_element_type=jnp.float32
            )
            total += bias_ref[...]
            if not is_raw:
                total += cross[0][:, at, :].reshape(8 * GROUP, TILE).astype(jnp.float32)
            out = 0.5 * total * (1.0 + lax.erf(total * math.sqrt(0.5)))
            out_ref[:, at, :] = out.astype(jnp.bfloat16).reshape(8, GROUP, TILE)

    w = pl.program_id(0)
    at = 0
    for p, is_raw in enumerate(raw):
        n = 2 if is_raw else 1
        cross = cross_refs[at : at + n]
        at += n
        if len(raw) == 1:
            one(cross, is_raw)
            return

        @pl.when((w >= (ends[p - 1] if p else 0)) & (w < ends[p]))
        def _(cross=cross, is_raw=is_raw):
            one(cross, is_raw)


def last(begin, rb, back_cols, image, sibling, cross, kron, bias_rows, so_far):
    chan, rows, width = image.shape
    first = begin // TILE
    ends = tuple(np.cumsum([c[0].shape[2] // TILE for c in cross]).tolist())
    raw = tuple(len(c) == 2 for c in cross)
    whole = pl.BlockSpec((chan, rows, TILE), lambda w: (0, 0, first + w))
    in_specs = [
        pl.BlockSpec((chan, rows, 2 * MY), lambda w: (0, 0, 0)),
        pl.BlockSpec((2 * MY, TILE), lambda w: (0, first + w)),
        whole,
        whole,
        pl.BlockSpec(kron.shape, lambda w: (0, 0)),
        pl.BlockSpec(bias_rows.shape, lambda w: (0, 0)),
    ]
    args = [rb, back_cols, image, sibling, kron, bias_rows]
    for p, c in enumerate(cross):
        lo, hi = (ends[p - 1] if p else 0), ends[p]
        for array in c:
            args.append(array)
            in_specs.append(
                pl.BlockSpec(
                    (chan, rows, TILE),
                    lambda w, lo=lo, hi=hi: (0, 0, jnp.clip(w - lo, 0, hi - lo - 1)),
                )
            )
    alias = {}
    if so_far is not None:
        in_specs.append(pl.BlockSpec(memory_space=pl.ANY))
        alias = {len(args): 0}
        args.append(so_far)
    return pl.pallas_call(
        functools.partial(last_kernel, ends, raw),
        grid=(ends[-1],),
        in_specs=in_specs,
        out_specs=whole,
        out_shape=jax.ShapeDtypeStruct((chan, rows, width), jnp.bfloat16),
        input_output_aliases=alias,
        compiler_params=pltpu.CompilerParams(vmem_limit_bytes=VMEM),
        cost_estimate=pl.CostEstimate(
            flops=4 * 8 * rows * TILE * 512 * ends[-1],
            bytes_accessed=3 * 2**20 * ends[-1],
            transcendentals=0,
        ),
        name="last",
    )(*args)


def on_device(image, spec_weight, point_weight, bias):
    chan, rows, width = image.shape
    cols_np, rows_np = tables()
    fwd_cols = jnp.asarray(cols_np)
    back_cols = jnp.asarray(np.ascontiguousarray(cols_np.T))
    row_at = lax.axis_index(("yh", "zh"))
    row_tab = lax.dynamic_slice_in_dim(jnp.asarray(rows_np), row_at, 1, 1).reshape(
        8 * rows, 2 * MX
    )
    group, column = ("x", "zl"), ("x", "zh", "zl")

    def cut(src, j):
        return src[:, :, CUTS[j] : CUTS[j + 1]]

    def send(src):
        return lax.ppermute(src, "yl", PAIR)

    parts = len(CUTS) - 1
    cross = [send(cut(image, 0))]
    sibling = lax.ppermute(image, "core", PAIR)
    with jax.named_scope("point_weights"):
        me = lax.axis_index(("yl", "core"))
        kron = spread(point_weight, me, [me, me ^ 1, me ^ 2, me ^ 3], chan)
        kron_other = spread(point_weight, me ^ 2, [me, me ^ 1], chan)
        bias_rows = jnp.repeat(bias, GROUP)[:, None]

    with jax.named_scope("colspec"):
        colspec = jnp.dot(
            image.reshape(chan * rows, width), fwd_cols, preferred_element_type=jnp.float32
        )
        colspec = (colspec * (1.0 / math.sqrt(W))).astype(jnp.bfloat16)
    later, colspec = lax.optimization_barrier((image, colspec))
    cross += [send(cut(later, j)) for j in range(1, RAW)]
    with jax.named_scope("swap_rows"):
        line = lax.all_to_all(colspec.reshape(chan, rows, 2 * MY), group, 0, 0, tiled=True)
    line = line.reshape(8 * rows, 2 * MY)
    line, cross[0] = lax.optimization_barrier((line, cross[0]))
    with jax.named_scope("row_dft"):
        part = lax.dot_general(
            row_tab, line, (((0,), (0,)), ((), ())), preferred_element_type=jnp.float32
        )
        spec_re = part[:MX, :MY] + part[MX:, MY:]
        spec_im = part[:MX, MY:] - part[MX:, :MY]
        part = jnp.concatenate([spec_re, spec_im], -1) * (1.0 / math.sqrt(H))
        part = part.astype(jnp.bfloat16).reshape(32, 8, 2 * MY)
    with jax.named_scope("swap_modes"):
        part = lax.all_to_all(part, column, 0, 0, tiled=True)
    with jax.named_scope("products"):
        made = [
            product(CUTS[j], CUTS[j + 1], image, sibling, kron_other) for j in range(RAW, parts)
        ]
    part, kron, *made = lax.optimization_barrier((part, kron, *made))
    with jax.named_scope("sum_lines"):
        part = jnp.sum(part.reshape(4, 4, 2, 8, 2 * MY).astype(jnp.float32), 1)
        part = part.astype(jnp.bfloat16).reshape(8, 2, 4, 2 * MY).transpose(1, 0, 2, 3)
        part = jnp.broadcast_to(part[:, None], (2, 4, 8, 4, 2 * MY)).reshape(64, 4, 2 * MY)
    with jax.named_scope("gather_chan"):
        part = lax.all_to_all(part, ("yh", "yl", "core"), 0, 0, tiled=True)
        part, cross[1] = lax.optimization_barrier((part, cross[1]))
        zed = jnp.sum(part.reshape(2, 32, 4, 2 * MY).astype(jnp.float32), 0).astype(jnp.bfloat16)
    with jax.named_scope("mix"):
        zed_re = zed[..., :MY].astype(jnp.float32)
        zed_im = zed[..., MY:].astype(jnp.float32)
        wgt_re = spec_weight[0].astype(jnp.float32)
        wgt_im = spec_weight[1].astype(jnp.float32)
        mix_re = jnp.einsum("kiop,ikp->okp", wgt_re, zed_re) - jnp.einsum(
            "kiop,ikp->okp", wgt_im, zed_im
        )
        mix_im = jnp.einsum("kiop,ikp->okp", wgt_re, zed_im) + jnp.einsum(
            "kiop,ikp->okp", wgt_im, zed_re
        )
        mixed = jnp.concatenate([mix_re, mix_im], -1).astype(jnp.bfloat16)
    with jax.named_scope("join_halves"):
        other = lax.ppermute(mixed, "yh", PAIR)
        other, *made = lax.optimization_barrier((other, *made))
        cross += [send(c) for c in made]
        first = lax.axis_index("yh") == 0
        mixed = jnp.concatenate(
            [jnp.where(first, mixed, other), jnp.where(first, other, mixed)], 1
        )
        mixed = mixed.reshape(4, 1, 2, 8, 2 * MY)
        mixed = jnp.broadcast_to(mixed, (4, 4, 2, 8, 2 * MY)).reshape(32, 8, 2 * MY)
    with jax.named_scope("spread_modes"):
        modes = lax.all_to_all(mixed, column, 0, 0, tiled=True).reshape(MX, 2 * MY)
    modes, cross[RAW] = lax.optimization_barrier((modes, cross[RAW]))
    with jax.named_scope("rowback"):
        mode_re, mode_im = modes[:, :MY], modes[:, MY:]
        turned = jnp.concatenate([modes, jnp.concatenate([-mode_im, mode_re], 1)], 0)
        back = jnp.dot(row_tab, turned, preferred_element_type=jnp.float32)
        back = (back * (1.0 / math.sqrt(MX) / math.sqrt(MY))).astype(jnp.bfloat16)
        back = back.reshape(8, rows, 2 * MY)
    with jax.named_scope("swap_back"):
        back = lax.all_to_all(back, group, 0, 0, tiled=True)
    cross = [(c, lax.ppermute(c, "core", PAIR)) if j < RAW else (c,) for j, c in enumerate(cross)]
    out = None
    for lo, hi in ((0, parts - 1), (parts - 1, parts)):
        out = last(
            CUTS[lo], back, back_cols, image, sibling, cross[lo:hi], kron, bias_rows, out
        )
    return out


def solution(mesh):
    fine = Mesh(mesh.devices.reshape(4, 2, 4, 2, 2, 2), ("x", "yh", "zh", "zl", "yl", "core"))
    row, chan = ("x", "yh", "zh", "zl"), ("yl", "core")
    in_specs = (P(chan, row, None), P(None, row, None, chan, None), P(), P(chan))
    return jax.shard_map(
        on_device, mesh=fine, in_specs=in_specs, out_specs=P(chan, row, None), check_vma=False
    )
```

time: 207 us -> 130 us (0.63)
  waiting for transfers between devices: 107 us -> 50.5 us
  matrix products: 40.9 us -> 9.75 us
  Pallas kernels: 0 us -> 19.7 us
  local copies, waits for them, and re-layouts: 15.9 us -> 10 us
  blocking collectives: 5.43 us -> 0 us
  starting transfers between devices: 33.2 us -> 35.4 us
    ppermute x8 -> x7, waiting for transfers between devices: 76.1 us -> 16.9 us  [the longest x4 11.9 us: send(): return lax.ppermute(src, 'yl', PAIR)]
    dot_general x2, matrix products: 30.5 us -> 2.21 us  [spread(): full = jnp.dot(full, jnp.asarray(wide, jnp.bfloat16))]
    pallas_call x0 -> x4, Pallas kernels: none -> 19.7 us  [the longest x2 14.3 us: last(): pl.pallas_call(functools.partial(last_kernel, ends, raw), grid=(ends[-1],...]
    unnamed x9 -> x20, local copies, waits for them, and re-layouts: 6.57 us -> 0.85 us
    all_gather x1 -> x0, blocking collectives: 5.43 us -> none  [on_device(): zed = lax.all_gather(spectrum, ('yl', 'core'), axis=0, tiled=True)]
    convert_element_type x1 -> x0, local copies, waits for them, and re-layouts: 4.31 us -> none  [on_device(): return jax.nn.gelu(total, approximate=False).astype(jnp.bfloat16)]
    all_to_all x4 -> x5, waiting for transfers between devices: 31.3 us -> 33.6 us  [the longest x1 10.5 us: on_device(): modes = lax.all_to_all(mixed, column, 0, 0, tiled=True).reshape(MX, 2 * MY)]
    all_to_all x4 -> x5, starting transfers between devices: 29.2 us -> 31.2 us  [the longest x1 11.2 us: on_device(): part = lax.all_to_all(part, column, 0, 0, tiled=True)]
  transfers between devices with their start and end apart: 13 -> 13, of which waited for: 7 -> 9; matrix products, arithmetic and copies ran while one was open for 9% -> 15% of each run, Pallas kernels for 0% -> 12%
where the time goes in v2:
time: 130 us; the launch traced here: 128 us
  waiting for transfers between devices  50.5 us (39%)
  starting transfers between devices  35.4 us (27%)
  Pallas kernels  19.7 us (15%)
  local copies, waits for them, and re-layouts  10 us (8%)
  matrix products  9.75 us (8%)
  other arithmetic  2.78 us (2%)
    pallas_call x2, Pallas kernels, last(): pl.pallas_call(functools.partial(last_kernel, ends, raw), grid=(ends[-1],...  14.3 us
    ppermute x4, waiting for transfers between devices, send(): return lax.ppermute(src, 'yl', PAIR)  11.9 us
    all_to_all x1, starting transfers between devices, on_device(): part = lax.all_to_all(part, column, 0, 0, tiled=True)  11.2 us
    all_to_all x1, waiting for transfers between devices, on_device(): modes = lax.all_to_all(mixed, column, 0, 0, tiled=True).reshape(MX, 2 * MY)  10.5 us
    all_to_all x1, waiting for transfers between devices, on_device(): part = lax.all_to_all(part, ('yh', 'yl', 'core'), 0, 0, tiled=True)  7.51 us
    all_to_all x1, waiting for transfers between devices, on_device(): back = lax.all_to_all(back, group, 0, 0, tiled=True)  6.16 us
    dot_general x1, matrix products, on_device(): jnp.dot(image.reshape(chan * rows, width), fwd_cols, preferred_element_ty...  5.84 us
    all_to_all x1, starting transfers between devices, on_device(): lax.all_to_all(colspec.reshape(chan, rows, 2 * MY), group, 0, 0, tiled=True)  5.76 us
  transfers between devices with their start and end apart: 13, of which 9 were waited for; matrix products, arithmetic and copies ran while one was open for 15% of the time, Pallas kernels for 12%

profile of v2, /device:TPU:32, one launch (start us, length us, event | category | flops | bytes accessed | tf_op | source)
XLA Modules:
  0.0 128.4 jit_solution(934539346130180571)
XLA Ops:
  0.0 2.3 %slice.36 = bf16[8,64,1024]{2,1,0:T(8,128)(2,1)} slice(bf16[8,64,4096]{2,1,0:T(8,128)(2,1)} %refs_2_.3), slice={[0:8], [0:64], [0:1024]} | slice | bytes 2097152 | tf_op jit(solution)/shard_map/slice | solution.py:182
  2.3 1.6 %collective-permute-start = (bf16[8,64,1024]{2,1,0:T(8,128)(2,1)}, bf16[8,64,1024]{2,1,0:T(8,128)(2,1)S(1)}, u32[]{:S(2)}, u32[]{:S(2)}) collective-permute-start(bf16[8,64,1024]{2,1,0:T(8,128)(2,1)} %slice.36), channel_id=1, source_target_pairs={{0,2},{2,0},{1,3},{3,1},{4,6},{6,4},{5,7},{7,5},{8,10},{10,8},{9,1... | collective-permute-start | bytes 3145736 | tf_op jit(solution)/shard_map/ppermute | solution.py:185
  3.8 5.8 %fusion.2 = bf16[512,512]{0,1:T(8,128)(2,1)S(1)} fusion(bf16[4096,512]{1,0:T(8,128)(2,1)} %constant.115.clone, bf16[512,4096]{1,0:T(8,128)(2,1)} %bitcast.57), kind=kOutput, calls=%fused_computation.8 | convolution fusion | flops 2148007936 | bytes 8912896 | tf_op jit(solution)/shard_map/colspec/dot_general | solution.py:197
  9.7 1.0 copy.35
  10.7 5.8 %all-to-all-start = ((bf16[8,64,512]{2,1,0:T(8,128)(2,1)}), bf16[8,64,512]{2,1,0:T(8,128)(2,1)S(1)}, u32[]{:S(2)}, u32[]{:S(2)}) async-start(bf16[8,64,512]{2,1,0:T(8,128)(2,1)} %bitcast.11), calls=%async_computation | async-start | bytes 1048576 | tf_op jit(solution)/shard_map/swap_rows/all_to_all | solution.py:204
  16.5 2.4 %slice.41 = bf16[8,64,1024]{2,1,0:T(8,128)(2,1)} slice(bf16[8,64,4096]{2,1,0:T(8,128)(2,1)} %refs_2_.3), slice={[0:8], [0:64], [1024:2048]} | slice | bytes 2097152 | tf_op jit(solution)/shard_map/slice | solution.py:182
  19.4 1.1 constant_dynamic-slice_fusion
  20.5 5.3 %all-to-all-done = bf16[8,64,512]{2,1,0:T(8,128)(2,1)S(1)} async-done(((bf16[8,64,512]{2,1,0:T(8,128)(2,1)}), bf16[8,64,512]{2,1,0:T(8,128)(2,1)S(1)}, u32[]{:S(2)}, u32[]{:S(2)}) %all-to-all-start) | async-done | bytes 524320 | tf_op jit(solution)/shard_map/swap_rows/all_to_all | solution.py:204
  25.8 2.7 %collective-permute-done.refs_6_ = bf16[8,64,1024]{2,1,0:T(8,128)(2,1)S(1)} collective-permute-done((bf16[8,64,1024]{2,1,0:T(8,128)(2,1)}, bf16[8,64,1024]{2,1,0:T(8,128)(2,1)S(1)}, u32[]{:S(2)}, u32[]{:S(2)}) %collective-permute-start) | collective-permute-done | bytes 1048608 | tf_op jit(solution)/shard_map/ppermute | solution.py:185
  29.0 0.7 fusion.11
  29.7 11.2 %all-to-all-start.1 = ((bf16[32,8,512]{2,1,0:T(8,128)(2,1)}), bf16[32,8,512]{2,1,0:T(8,128)(2,1)S(1)}, u32[]{:S(2)}, u32[]{:S(2)}) async-start(bf16[32,8,512]{2,1,0:T(8,128)(2,1)} %fusion.11), calls=%async_computation.1 | async-start | bytes 524288 | tf_op jit(solution)/shard_map/swap_modes/all_to_all | solution.py:216
  40.9 1.1 convolution_multiply_fusion.3.kron_ref
  42.0 1.1 convolution_multiply_fusion.2.refs_4_
  43.1 2.8 %product.3 = bf16[8,64,1024]{2,1,0:T(8,128)(2,1)} custom-call(bf16[8,64,4096]{2,1,0:T(8,128)(2,1)} %refs_2_.3, bf16[8,64,4096]{2,1,0:T(8,128)(2,1)} %collective-permute-done.1.sib_ref.refs_3_, bf16[128,256]{1,0:T(8,128)(2,1)} %convolution_multiply_fusion.3.kron_ref), custom_call_target="tpu_custom_call" | custom-call | flops 268435456 | bytes 3145728 | tf_op jit(solution)/shard_map/products/product/pallas_call | solution.py:68
  45.9 2.7 %product.2 = bf16[8,64,1024]{2,1,0:T(8,128)(2,1)} custom-call(bf16[8,64,4096]{2,1,0:T(8,128)(2,1)} %refs_2_.3, bf16[8,64,4096]{2,1,0:T(8,128)(2,1)} %collective-permute-done.1.sib_ref.refs_3_, bf16[128,256]{1,0:T(8,128)(2,1)} %convolution_multiply_fusion.3.kron_ref), custom_call_target="tpu_custom_call" | custom-call | flops 268435456 | bytes 3145728 | tf_op jit(solution)/shard_map/products/product/pallas_call | solution.py:68
  48.6 4.1 %all-to-all-done.1 = bf16[32,8,512]{2,1,0:T(8,128)(2,1)S(1)} async-done(((bf16[32,8,512]{2,1,0:T(8,128)(2,1)}), bf16[32,8,512]{2,1,0:T(8,128)(2,1)S(1)}, u32[]{:S(2)}, u32[]{:S(2)}) %all-to-all-start.1) | async-done | bytes 262176 | tf_op jit(solution)/shard_map/swap_modes/all_to_all | solution.py:216
  52.8 0.8 broadcast_in_dim.16
  53.6 4.5 %all-to-all-start.2 = ((bf16[64,4,512]{2,1,0:T(4,128)(2,1)}), bf16[64,4,512]{2,1,0:T(4,128)(2,1)S(1)}, u32[]{:S(2)}, u32[]{:S(2)}) async-start(bf16[64,4,512]{2,1,0:T(4,128)(2,1)} %bitcast.17), calls=%async_computation.2 | async-start | bytes 524288 | tf_op jit(solution)/shard_map/gather_chan/all_to_all | solution.py:227
  58.1 7.5 %all-to-all-done.2 = bf16[64,4,512]{2,1,0:T(4,128)(2,1)S(1)} async-done(((bf16[64,4,512]{2,1,0:T(4,128)(2,1)}), bf16[64,4,512]{2,1,0:T(4,128)(2,1)S(1)}, u32[]{:S(2)}, u32[]{:S(2)}) %all-to-all-start.2) | async-done | bytes 262176 | tf_op jit(solution)/shard_map/gather_chan/all_to_all | solution.py:227
  65.9 1.6 %fusion.7 = (f32[4,256,8]{1,2,0:T(8,128)S(1)}, f32[4,256,8]{1,2,0:T(8,128)S(1)}, f32[4,256,8]{1,2,0:T(8,128)S(1)}, f32[4,256,8]{1,2,0:T(8,128)S(1)}) fusion(f32[4,256,32]{1,2,0:T(8,128)S(1)} %get-tuple-element.56, bf16[2,4,32,8,256]{4,3,2,1,0:T(8,128)(2,1)} %param.14, f32[4,256,32]{1,2,0:T(8,128)S(1)} %get-tuple-element.55), kind=kLoop, calls=%fused_computation.13 | loop fusion | flops 2588672 | bytes 1441792
  68.0 5.0 %collective-permute-done.3 = bf16[8,4,512]{2,1,0:T(4,128)(2,1)S(1)} collective-permute-done((bf16[8,4,512]{2,1,0:T(4,128)(2,1)S(1)}, bf16[8,4,512]{2,1,0:T(4,128)(2,1)S(1)}, u32[]{:S(2)}, u32[]{:S(2)}) %collective-permute-start.3) | collective-permute-done | bytes 32800 | tf_op jit(solution)/shard_map/join_halves/ppermute | solution.py:243
  73.7 0.7 broadcast_in_dim.18
  74.4 5.7 %all-to-all-start.3 = ((bf16[32,8,512]{2,1,0:T(8,128)(2,1)}), bf16[32,8,512]{2,1,0:T(8,128)(2,1)S(1)}, u32[]{:S(2)}, u32[]{:S(2)}) async-start(bf16[32,8,512]{2,1,0:T(8,128)(2,1)} %bitcast.28), calls=%async_computation.3 | async-start | bytes 524288 | tf_op jit(solution)/shard_map/spread_modes/all_to_all | solution.py:253
  80.7 10.5 %all-to-all-done.3 = bf16[32,8,512]{2,1,0:T(8,128)(2,1)S(1)} async-done(((bf16[32,8,512]{2,1,0:T(8,128)(2,1)}), bf16[32,8,512]{2,1,0:T(8,128)(2,1)S(1)}, u32[]{:S(2)}, u32[]{:S(2)}) %all-to-all-start.3) | async-done | bytes 262176 | tf_op jit(solution)/shard_map/spread_modes/all_to_all | solution.py:253
  91.1 5.6 %collective-permute-done.4.refs_10_ = bf16[8,64,1024]{2,1,0:T(8,128)(2,1)} collective-permute-done((bf16[8,64,1024]{2,1,0:T(8,128)(2,1)}, bf16[8,64,1024]{2,1,0:T(8,128)(2,1)}, u32[]{:S(2)}, u32[]{:S(2)}) %collective-permute-start.4) | collective-permute-done | bytes 1048608 | tf_op jit(solution)/shard_map/join_halves/ppermute | solution.py:185
  96.7 1.2 fusion.1
  98.0 4.1 %all-to-all-start.4 = ((bf16[8,64,512]{2,1,0:T(8,128)(2,1)}), bf16[8,64,512]{2,1,0:T(8,128)(2,1)S(1)}, u32[]{:S(2)}, u32[]{:S(2)}) async-start(bf16[8,64,512]{2,1,0:T(8,128)(2,1)} %bitcast.30), calls=%async_computation.4 | async-start | bytes 1048576 | tf_op jit(solution)/shard_map/swap_back/all_to_all | solution.py:262
  103.5 6.2 %all-to-all-done.4.refs_0_ = bf16[8,64,512]{2,1,0:T(8,128)(2,1)S(1)} async-done(((bf16[8,64,512]{2,1,0:T(8,128)(2,1)}), bf16[8,64,512]{2,1,0:T(8,128)(2,1)S(1)}, u32[]{:S(2)}, u32[]{:S(2)}) %all-to-all-start.4) | async-done | bytes 524320 | tf_op jit(solution)/shard_map/swap_back/all_to_all | solution.py:262
  109.6 0.8 copy-done
  110.4 10.4 %last.2.refs_7_ = bf16[8,64,4096]{2,1,0:T(8,128)(2,1)} custom-call(bf16[8,64,512]{2,1,0:T(8,128)(2,1)} %copy-done, bf16[512,4096]{1,0:T(8,128)(2,1)} %constant.116.clone.refs_1_, bf16[8,64,4096]{2,1,0:T(8,128)(2,1)} %refs_2_.3, bf16[8,64,4096]{2,1,0:T(8,128)(2,1)} %collective-permute-done.1.sib_ref.refs_3_, ...), custom_call_target="tpu_custom_call" | custom-call | flops 3221225472 | bytes 18874368 | tf_op jit(solution)/shard_map/last/pallas_call | solution.py:153
  120.8 3.7 %collective-permute-done.5.refs_6_ = bf16[8,64,1024]{2,1,0:T(8,128)(2,1)} collective-permute-done((bf16[8,64,1024]{2,1,0:T(8,128)(2,1)}, bf16[8,64,1024]{2,1,0:T(8,128)(2,1)}, u32[]{:S(2)}, u32[]{:S(2)}) %collective-permute-start.5) | collective-permute-done | bytes 1048608 | tf_op jit(solution)/shard_map/join_halves/ppermute | solution.py:185
  124.5 4.0 %last.3 = bf16[8,64,4096]{2,1,0:T(8,128)(2,1)} custom-call(bf16[8,64,512]{2,1,0:T(8,128)(2,1)} %copy-done, bf16[512,4096]{1,0:T(8,128)(2,1)} %constant.116.clone.refs_1_, bf16[8,64,4096]{2,1,0:T(8,128)(2,1)} %refs_2_.3, bf16[8,64,4096]{2,1,0:T(8,128)(2,1)} %collective-permute-done.1.sib_ref.refs_3_, ...), custom_call_target="tpu_custom_call", output_to_operand_aliasing={{}: (7, {})} | custom-call | flops 1073741824 | bytes 6291456 | tf_op jit(solution)/shard_map/last/pallas_call | solution.py:153
  (47 shorter events, 4.6 us)
Async XLA Ops:
  0.0 43.1 %collective-permute-start.1 = (bf16[8,64,4096]{2,1,0:T(8,128)(2,1)}, bf16[8,64,4096]{2,1,0:T(8,128)(2,1)}, u32[]{:S(2)}, u32[]{:S(2)}) collective-permute-start(bf16[8,64,4096]{2,1,0:T(8,128)(2,1)} %refs_2_.3), channel_id=1, source_target_pairs={{0,1},{1,0},{2,3},{3,2},{4,5},{5,4},{6,7},{7,6},{8,9},{9,8},{10,11... | collective-permute-start | bytes 12582920 | tf_op jit(solution)/shard_map/ppermute | solution.py:189
  2.3 26.2 %collective-permute-start = (bf16[8,64,1024]{2,1,0:T(8,128)(2,1)}, bf16[8,64,1024]{2,1,0:T(8,128)(2,1)S(1)}, u32[]{:S(2)}, u32[]{:S(2)}) collective-permute-start(bf16[8,64,1024]{2,1,0:T(8,128)(2,1)} %slice.36), channel_id=1, source_target_pairs={{0,2},{2,0},{1,3},{3,1},{4,6},{6,4},{5,7},{7,5},{8,10},{10,8},{9,1... | collective-permute-start | bytes 3145736 | tf_op jit(solution)/shard_map/ppermute | solution.py:185
  9.7 9.6 %copy-start.7 = (bf16[32,32]{1,0:T(8,128)(2,1)S(1)}, bf16[32,32]{1,0:T(8,128)(2,1)}, u32[]{:S(2)}) copy-start(bf16[32,32]{1,0:T(8,128)(2,1)} %param.15) | copy-start | bytes 6148
  10.7 15.1 %all-to-all-start = ((bf16[8,64,512]{2,1,0:T(8,128)(2,1)}), bf16[8,64,512]{2,1,0:T(8,128)(2,1)S(1)}, u32[]{:S(2)}, u32[]{:S(2)}) async-start(bf16[8,64,512]{2,1,0:T(8,128)(2,1)} %bitcast.11), calls=%async_computation | async-start | bytes 1048576 | tf_op jit(solution)/shard_map/swap_rows/all_to_all | solution.py:204
  16.5 24.4 %copy-start.4 = (bf16[128,8]{1,0:T(8,128)(2,1)S(1)}, bf16[128,8]{1,0:T(8,128)(2,1)}, u32[]{:S(2)}) copy-start(bf16[128,8]{1,0:T(8,128)(2,1)} %constant.118.clone) | copy-start | bytes 6148
  16.5 24.4 %copy-start.5 = (bf16[128,256]{1,0:T(8,128)(2,1)S(1)}, bf16[128,256]{1,0:T(8,128)(2,1)}, u32[]{:S(2)}) copy-start(bf16[128,256]{1,0:T(8,128)(2,1)} %constant.122.clone) | copy-start | bytes 196612
  16.5 24.4 %copy-start.8 = (bf16[16,256]{1,0:T(8,128)(2,1)S(1)}, bf16[16,256]{1,0:T(8,128)(2,1)}, u32[]{:S(2)}) copy-start(bf16[16,256]{1,0:T(8,128)(2,1)} %constant.121.clone) | copy-start | bytes 24580
  16.5 25.5 %copy-start.3 = (bf16[128,512]{1,0:T(8,128)(2,1)S(1)}, bf16[128,512]{1,0:T(8,128)(2,1)}, u32[]{:S(2)}) copy-start(bf16[128,512]{1,0:T(8,128)(2,1)} %constant.120.clone) | copy-start | bytes 393220
  16.5 25.5 %copy-start.6 = (bf16[32,512]{1,0:T(8,128)(2,1)S(1)}, bf16[32,512]{1,0:T(8,128)(2,1)}, u32[]{:S(2)}) copy-start(bf16[32,512]{1,0:T(8,128)(2,1)} %constant.119.clone) | copy-start | bytes 98308
  18.9 39.2 %collective-permute-start.2 = (bf16[8,64,1024]{2,1,0:T(8,128)(2,1)}, bf16[8,64,1024]{2,1,0:T(8,128)(2,1)S(1)}, u32[]{:S(2)}, u32[]{:S(2)}) collective-permute-start(bf16[8,64,1024]{2,1,0:T(8,128)(2,1)} %slice.41), channel_id=1, source_target_pairs={{0,2},{2,0},{1,3},{3,1},{4,6},{6,4},{5,7},{7,5},{8,10},{10,8},{9,1... | collective-permute-start | bytes 3145736 | tf_op jit(solution)/shard_map/ppermute | solution.py:185
  28.4 51.6 %copy-start.1 = (bf16[8,64,1024]{2,1,0:T(8,128)(2,1)}, bf16[8,64,1024]{2,1,0:T(8,128)(2,1)S(1)}, u32[]{:S(2)}) copy-start(bf16[8,64,1024]{2,1,0:T(8,128)(2,1)S(1)} %collective-permute-done.refs_6_) | copy-start | bytes 3145732
  29.7 23.0 %all-to-all-start.1 = ((bf16[32,8,512]{2,1,0:T(8,128)(2,1)}), bf16[32,8,512]{2,1,0:T(8,128)(2,1)S(1)}, u32[]{:S(2)}, u32[]{:S(2)}) async-start(bf16[32,8,512]{2,1,0:T(8,128)(2,1)} %fusion.11), calls=%async_computation.1 | async-start | bytes 524288 | tf_op jit(solution)/shard_map/swap_modes/all_to_all | solution.py:216
  53.6 12.0 %all-to-all-start.2 = ((bf16[64,4,512]{2,1,0:T(4,128)(2,1)}), bf16[64,4,512]{2,1,0:T(4,128)(2,1)S(1)}, u32[]{:S(2)}, u32[]{:S(2)}) async-start(bf16[64,4,512]{2,1,0:T(4,128)(2,1)} %bitcast.17), calls=%async_computation.2 | async-start | bytes 524288 | tf_op jit(solution)/shard_map/gather_chan/all_to_all | solution.py:227
  58.0 44.6 %copy-start.9 = (f32[8]{0:T(128)S(1)}, f32[8]{0:T(128)}, u32[]{:S(2)}) copy-start(f32[8]{0:T(128)} %param.16) | copy-start | bytes 100
  58.0 51.6 %copy-start.2 = (bf16[8,64,1024]{2,1,0:T(8,128)(2,1)}, bf16[8,64,1024]{2,1,0:T(8,128)(2,1)S(1)}, u32[]{:S(2)}) copy-start(bf16[8,64,1024]{2,1,0:T(8,128)(2,1)S(1)} %collective-permute-done.2.refs_8_) | copy-start | bytes 3145732
  67.5 5.5 %collective-permute-start.3 = (bf16[8,4,512]{2,1,0:T(4,128)(2,1)S(1)}, bf16[8,4,512]{2,1,0:T(4,128)(2,1)S(1)}, u32[]{:S(2)}, u32[]{:S(2)}) collective-permute-start(bf16[8,4,512]{2,1,0:T(4,128)(2,1)S(1)} %pad_maximum_fusion.1), channel_id=1, source_target_pairs={{0,32},{32,0},{1,33},{33,1},{2,34},{34,2},{3,35},{35,3},{4,36},{36... | collective-permute-start | bytes 98312 | tf_op jit(solution)/shard_map/join_halves/ppermute | solution.py:243
  73.0 23.7 %collective-permute-start.4 = (bf16[8,64,1024]{2,1,0:T(8,128)(2,1)}, bf16[8,64,1024]{2,1,0:T(8,128)(2,1)}, u32[]{:S(2)}, u32[]{:S(2)}) collective-permute-start(bf16[8,64,1024]{2,1,0:T(8,128)(2,1)} %product.2), channel_id=1, source_target_pairs={{0,2},{2,0},{1,3},{3,1},{4,6},{6,4},{5,7},{7,5},{8,10},{10,8},{9,1... | collective-permute-start | bytes 3145736 | tf_op jit(solution)/shard_map/join_halves/ppermute | solution.py:185
  74.4 16.7 %all-to-all-start.3 = ((bf16[32,8,512]{2,1,0:T(8,128)(2,1)}), bf16[32,8,512]{2,1,0:T(8,128)(2,1)S(1)}, u32[]{:S(2)}, u32[]{:S(2)}) async-start(bf16[32,8,512]{2,1,0:T(8,128)(2,1)} %bitcast.28), calls=%async_computation.3 | async-start | bytes 524288 | tf_op jit(solution)/shard_map/spread_modes/all_to_all | solution.py:253
  80.1 23.4 %collective-permute-start.6 = (bf16[8,64,1024]{2,1,0:T(8,128)(2,1)S(1)}, bf16[8,64,1024]{2,1,0:T(8,128)(2,1)}, u32[]{:S(2)}, u32[]{:S(2)}) collective-permute-start(bf16[8,64,1024]{2,1,0:T(8,128)(2,1)S(1)} %collective-permute-done.refs_6_), channel_id=1, source_target_pairs={{0,1},{1,0},{2,3},{3,2},{4,5},{5,4},{6,7},{7,6},{8,9},{9,8},{10,11... | collective-permute-start | bytes 3145736 | tf_op jit(solution)/shard_map/ppermute | solution.py:263
  80.2 23.3 %collective-permute-start.7 = (bf16[8,64,1024]{2,1,0:T(8,128)(2,1)S(1)}, bf16[8,64,1024]{2,1,0:T(8,128)(2,1)}, u32[]{:S(2)}, u32[]{:S(2)}) collective-permute-start(bf16[8,64,1024]{2,1,0:T(8,128)(2,1)S(1)} %collective-permute-done.2.refs_8_), channel_id=1, source_target_pairs={{0,1},{1,0},{2,3},{3,2},{4,5},{5,4},{6,7},{7,6},{8,9},{9,8},{10,11... | collective-permute-start | bytes 3145736 | tf_op jit(solution)/shard_map/ppermute | solution.py:263
  98.0 11.7 %all-to-all-start.4 = ((bf16[8,64,512]{2,1,0:T(8,128)(2,1)}), bf16[8,64,512]{2,1,0:T(8,128)(2,1)S(1)}, u32[]{:S(2)}, u32[]{:S(2)}) async-start(bf16[8,64,512]{2,1,0:T(8,128)(2,1)} %bitcast.30), calls=%async_computation.4 | async-start | bytes 1048576 | tf_op jit(solution)/shard_map/swap_back/all_to_all | solution.py:262
  102.1 22.4 %collective-permute-start.5 = (bf16[8,64,1024]{2,1,0:T(8,128)(2,1)}, bf16[8,64,1024]{2,1,0:T(8,128)(2,1)}, u32[]{:S(2)}, u32[]{:S(2)}) collective-permute-start(bf16[8,64,1024]{2,1,0:T(8,128)(2,1)} %product.3), channel_id=1, source_target_pairs={{0,2},{2,0},{1,3},{3,1},{4,6},{6,4},{5,7},{7,5},{8,10},{10,8},{9,1... | collective-permute-start | bytes 3145736 | tf_op jit(solution)/shard_map/join_halves/ppermute | solution.py:185
  109.6 0.8 copy-start

commit v3 on v1

v3 whole, which is shorter than its diff:
```python
import functools
import math

import jax
import jax.numpy as jnp
import ml_dtypes
import numpy as np
from jax import lax
from jax.experimental import pallas as pl
from jax.experimental.pallas import tpu as pltpu
from jax.sharding import Mesh, PartitionSpec as P

H = 4096
W = 4096
MX = 256
MY = 256
PAIR = [(0, 1), (1, 0)]
GROUP = 16
VMEM = 56 * 2**20
SMALL = 16 * 2**20
TILE = 512
RAW = 2048
RAW_CUTS = (0, 1024, RAW)


def wave_table(points, freqs, length):
    prod = np.mod(points[:, None] * freqs[None, :], length)
    one = np.arange(length).astype(np.float32) * np.float32(2.0 * math.pi / length)
    return np.cos(one)[prod], np.sin(one)[prod]


def tables():
    cos_w, sin_w = wave_table(np.arange(W), np.arange(MY), W)
    cols = np.concatenate([cos_w, -sin_w], 1)
    freq = np.arange(MX).reshape(4, 2, 8, 4).transpose(0, 2, 1, 3).reshape(-1) - MX // 2
    cos_h, sin_h = wave_table(np.arange(H), freq, H)
    rows = np.concatenate([cos_h, sin_h], 1).reshape(4, 8, 2 * 64, 2 * MX)
    return cols.astype(ml_dtypes.bfloat16), rows.astype(ml_dtypes.bfloat16)


def spread(point_weight, outputs, inputs, chan):
    mine = lax.dynamic_slice(point_weight, (outputs * chan, 0), (chan, 4 * chan))
    order = jnp.concatenate(
        [lax.dynamic_slice(mine, (0, i * chan), (chan, chan)) for i in inputs], 1
    )
    n = len(inputs) * chan
    tall = np.kron(np.eye(chan), np.ones((GROUP, 1)))
    wide = np.kron(np.eye(n), np.ones((1, GROUP)))
    same = np.tile(np.eye(GROUP), (chan, n))
    full = jnp.dot(jnp.asarray(tall, jnp.bfloat16), order)
    full = jnp.dot(full, jnp.asarray(wide, jnp.bfloat16))
    return full * jnp.asarray(same, jnp.bfloat16)


def stack(refs, at):
    return jnp.concatenate([r[:, at, :].reshape(-1, TILE) for r in refs], 0)


def block(chan, rows, lo=0, hi=None):
    if hi is None:
        return pl.BlockSpec((chan, rows, TILE), lambda w: (0, 0, w + lo))
    return pl.BlockSpec(
        (chan, rows, TILE), lambda w: (0, 0, jnp.clip(w - lo, 0, hi - lo - 1))
    )


def product_kernel(
    own_ref, sib_ref, kron_ref, soon_ref, late_ref, half_ref, next_ref, end_ref
):
    step = pl.program_id(0)
    for t, (mine_ref, place, theirs) in enumerate(
        (
            (soon_ref, 0, ((next_ref, 0, 8),)),
            (late_ref, 0, ((half_ref, 0, 4), (end_ref, 0, 4))),
            (late_ref, 1, ((end_ref, 4, 8),)),
            (late_ref, 2, ((end_ref, 12, 8),)),
        )
    ):

        @pl.when(step == t)
        def _(mine_ref=mine_ref, place=place, theirs=theirs):
            for g in range(own_ref.shape[1] // GROUP):
                at = pl.ds(g * GROUP, GROUP)
                total = jnp.dot(
                    kron_ref[...],
                    stack((own_ref, sib_ref), at),
                    preferred_element_type=jnp.float32,
                )
                total = total.astype(jnp.bfloat16).reshape(16, GROUP, TILE)
                mine_ref[:, at, pl.ds(place * TILE, TILE)] = total[:8]
                done = 8
                for ref, lo, n in theirs:
                    ref[lo : lo + n, at, :] = total[done : done + n]
                    done += n


def product(image, sibling, kron):
    chan, rows, width = image.shape
    first, tiles = RAW // TILE, (width - RAW) // TILE
    sizes = [(chan, TILE), (chan, 3 * TILE), (4, TILE), (8, TILE), (20, TILE)]
    return pl.pallas_call(
        product_kernel,
        grid=(tiles,),
        in_specs=[block(chan, rows, first)] * 2 + [pl.BlockSpec(kron.shape, lambda w: (0, 0))],
        out_specs=[pl.BlockSpec((n, rows, w), lambda w: (0, 0, 0)) for n, w in sizes],
        out_shape=[jax.ShapeDtypeStruct((n, rows, w), jnp.bfloat16) for n, w in sizes],
        compiler_params=pltpu.CompilerParams(vmem_limit_bytes=VMEM),
        cost_estimate=pl.CostEstimate(
            flops=4 * 8 * rows * TILE * 256 * tiles,
            bytes_accessed=2**21 * tiles,
            transcendentals=0,
        ),
        name="product",
    )(image, sibling, kron)


def pointwise_kernel(own_ref, sib_ref, cross_ref, csib_ref, kron_ref, out_ref):
    for g in range(own_ref.shape[1] // GROUP):
        at = pl.ds(g * GROUP, GROUP)
        total = jnp.dot(
            kron_ref[...],
            stack((own_ref, sib_ref, cross_ref, csib_ref), at),
            preferred_element_type=jnp.float32,
        )
        out_ref[:, at, :] = total.astype(jnp.bfloat16).reshape(8, GROUP, TILE)


def pointwise(begin, image, sibling, cross, kron):
    chan, rows, width = cross.shape
    steps = width // TILE
    return pl.pallas_call(
        pointwise_kernel,
        grid=(steps,),
        in_specs=[block(chan, rows, begin // TILE)] * 2
        + [block(chan, rows)] * 2
        + [pl.BlockSpec(kron.shape, lambda w: (0, 0))],
        out_specs=block(chan, rows),
        out_shape=jax.ShapeDtypeStruct(cross.shape, jnp.bfloat16),
        compiler_params=pltpu.CompilerParams(vmem_limit_bytes=VMEM),
        cost_estimate=pl.CostEstimate(
            flops=2 * 8 * rows * width * 512,
            bytes_accessed=5 * 2**19 * steps,
            transcendentals=0,
        ),
        name="pointwise",
    )(image, sibling, cross, lax.ppermute(cross, "core", PAIR), kron)


def finish(rb_ref, back_ref, bias_ref, terms, out_ref, place=0):
    cols = pl.ds(place * TILE, TILE)
    for g in range(rb_ref.shape[1] // GROUP):
        at = pl.ds(g * GROUP, GROUP)
        total = jnp.dot(
            rb_ref[:, at, :].reshape(8 * GROUP, 2 * MY),
            back_ref[:, cols],
            preferred_element_type=jnp.float32,
        )
        for term in terms:
            term = [
                ref[lo : lo + n, at, pl.ds(c, TILE)].reshape(n * GROUP, TILE)
                for ref, lo, n, c in term
            ]
            total += jnp.concatenate(term, 0).astype(jnp.float32)
        total += bias_ref[...]
        out = 0.5 * total * (1.0 + lax.erf(total * math.sqrt(0.5)))
        out_ref[:, at, :] = out.astype(jnp.bfloat16).reshape(8, GROUP, TILE)


def most_kernel(rb_ref, back_ref, bias_ref, first_ref, second_ref, soon_ref, next_ref, out_ref):
    column = pl.program_id(0) * TILE

    @pl.when(column < RAW_CUTS[1])
    def _():
        finish(rb_ref, back_ref, bias_ref, ([(first_ref, 0, 8, 0)],), out_ref)

    @pl.when((column >= RAW_CUTS[1]) & (column < RAW))
    def _():
        finish(rb_ref, back_ref, bias_ref, ([(second_ref, 0, 8, 0)],), out_ref)

    @pl.when(column >= RAW)
    def _():
        terms = ([(soon_ref, 0, 8, 0)], [(next_ref, 0, 8, 0)])
        finish(rb_ref, back_ref, bias_ref, terms, out_ref)


def most(rb, back_cols, bias_rows, first, second, soon, following):
    chan, rows, _ = rb.shape
    width = back_cols.shape[1]
    cuts = [c // TILE for c in RAW_CUTS]

    def still(array):
        return pl.BlockSpec(array.shape, lambda w: (0,) * array.ndim)

    return pl.pallas_call(
        most_kernel,
        grid=(cuts[2] + 1,),
        in_specs=[
            still(rb),
            pl.BlockSpec((2 * MY, TILE), lambda w: (0, w)),
            still(bias_rows),
            block(chan, rows, 0, cuts[1]),
            block(chan, rows, cuts[1], cuts[2]),
            still(soon),
            still(following),
        ],
        out_specs=block(chan, rows),
        out_shape=jax.ShapeDtypeStruct((chan, rows, width), jnp.bfloat16),
        compiler_params=pltpu.CompilerParams(vmem_limit_bytes=VMEM),
        cost_estimate=pl.CostEstimate(flops=1, bytes_accessed=1, transcendentals=0),
        name="most",
    )(rb, back_cols, bias_rows, first, second, soon, following)


def rest_kernel(rb_ref, back_ref, bias_ref, late_ref, half_ref, end_ref, so_far_ref, out_ref):
    others = (
        [(half_ref, 0, 4, 0), (end_ref, 0, 4, 0)],
        [(end_ref, 4, 8, 0)],
        [(end_ref, 12, 8, 0)],
    )
    for t, other in enumerate(others):

        @pl.when(pl.program_id(0) == t)
        def _(t=t, other=other):
            terms = ([(late_ref, 0, 8, t * TILE)], other)
            finish(rb_ref, back_ref, bias_ref, terms, out_ref, t)


def rest(rb, back_tiles, bias_rows, late, half, end, so_far):
    chan, rows, width = so_far.shape
    whole = pl.BlockSpec(memory_space=pltpu.VMEM)
    return pl.pallas_call(
        rest_kernel,
        grid=(3,),
        in_specs=[whole] * 6 + [pl.BlockSpec(memory_space=pl.ANY)],
        out_specs=block(chan, rows, width // TILE - 3),
        out_shape=jax.ShapeDtypeStruct(so_far.shape, jnp.bfloat16),
        input_output_aliases={6: 0},
        compiler_params=pltpu.CompilerParams(vmem_limit_bytes=SMALL),
        cost_estimate=pl.CostEstimate(flops=1, bytes_accessed=1, transcendentals=0),
        name="rest",
    )(rb, back_tiles, bias_rows, late, half, end, so_far)


def on_device(image, spec_weight, point_weight, bias):
    chan, rows, width = image.shape
    cols_np, rows_np = tables()
    fwd_cols = jnp.asarray(cols_np)
    back_cols = jnp.asarray(np.ascontiguousarray(cols_np.T))
    row_at = lax.axis_index(("yh", "zh"))
    row_tab = lax.dynamic_slice_in_dim(jnp.asarray(rows_np), row_at, 1, 1).reshape(
        8 * rows, 2 * MX
    )
    group, column = ("x", "zl"), ("x", "zh", "zl")

    def send(src):
        return lax.ppermute(src, "yl", PAIR)

    def raw(src, j):
        return src[:, :, RAW_CUTS[j] : RAW_CUTS[j + 1]]

    first, later = lax.optimization_barrier((raw(image, 0), image))
    cross = [send(first)]
    sibling = lax.ppermute(later, "core", PAIR)
    with jax.named_scope("point_weights"):
        me = lax.axis_index(("yl", "core"))
        kron = spread(point_weight, me, [me, me ^ 1, me ^ 2, me ^ 3], chan)
        kron_other = spread(point_weight, me ^ 2, [me, me ^ 1], chan)
        kron_both = jnp.concatenate([kron[:, : kron.shape[1] // 2], kron_other], 0)
        bias_rows = jnp.repeat(bias, GROUP)[:, None]

    with jax.named_scope("colspec"):
        colspec = jnp.dot(
            image.reshape(chan * rows, width), fwd_cols, preferred_element_type=jnp.float32
        )
        colspec = (colspec * (1.0 / math.sqrt(W))).astype(jnp.bfloat16)
    later, _ = lax.optimization_barrier((image, colspec))
    cross += [send(raw(later, j)) for j in range(1, len(RAW_CUTS) - 1)]
    with jax.named_scope("swap_rows"):
        line = lax.all_to_all(colspec.reshape(chan, rows, 2 * MY), group, 0, 0, tiled=True)
    line = line.reshape(8 * rows, 2 * MY)
    line, cross[0] = lax.optimization_barrier((line, cross[0]))
    with jax.named_scope("row_dft"):
        part = lax.dot_general(
            row_tab, line, (((0,), (0,)), ((), ())), preferred_element_type=jnp.float32
        )
        spec_re = part[:MX, :MY] + part[MX:, MY:]
        spec_im = part[:MX, MY:] - part[MX:, :MY]
        part = jnp.concatenate([spec_re, spec_im], -1) * (1.0 / math.sqrt(H))
        part = part.astype(jnp.bfloat16).reshape(32, 8, 2 * MY)
    with jax.named_scope("swap_modes"):
        part = lax.all_to_all(part, column, 0, 0, tiled=True)
    with jax.named_scope("products"):
        soon, late, half, following, end = product(image, sibling, kron_both)
    part, kron, bias_rows, soon, late, half, following, end = lax.optimization_barrier(
        (part, kron, bias_rows, soon, late, half, following, end)
    )
    half = send(half)
    with jax.named_scope("sum_lines"):
        part = jnp.sum(part.reshape(4, 4, 2, 8, 2 * MY).astype(jnp.float32), 1)
        part = part.astype(jnp.bfloat16).reshape(8, 2, 4, 2 * MY).transpose(1, 0, 2, 3)
        part = jnp.broadcast_to(part[:, None], (2, 4, 8, 4, 2 * MY)).reshape(64, 4, 2 * MY)
    with jax.named_scope("gather_chan"):
        part = lax.all_to_all(part, ("yh", "yl", "core"), 0, 0, tiled=True)
        part, cross = lax.optimization_barrier((part, cross))
        zed = jnp.sum(part.reshape(2, 32, 4, 2 * MY).astype(jnp.float32), 0).astype(jnp.bfloat16)
    with jax.named_scope("mix"):
        zed_re = zed[..., :MY].astype(jnp.float32)
        zed_im = zed[..., MY:].astype(jnp.float32)
        wgt_re = spec_weight[0].astype(jnp.float32)
        wgt_im = spec_weight[1].astype(jnp.float32)
        mix_re = jnp.einsum("kiop,ikp->okp", wgt_re, zed_re) - jnp.einsum(
            "kiop,ikp->okp", wgt_im, zed_im
        )
        mix_im = jnp.einsum("kiop,ikp->okp", wgt_re, zed_im) + jnp.einsum(
            "kiop,ikp->okp", wgt_im, zed_re
        )
        mixed = jnp.concatenate([mix_re, mix_im], -1).astype(jnp.bfloat16)
    mixed, half = lax.optimization_barrier((mixed, half))
    with jax.named_scope("join_halves"):
        other = lax.ppermute(mixed, "yh", PAIR)
        other, following, end = lax.optimization_barrier((other, following, end))
        following, end = send(following), send(end)
        first = lax.axis_index("yh") == 0
        mixed = jnp.concatenate(
            [jnp.where(first, mixed, other), jnp.where(first, other, mixed)], 1
        )
        mixed = mixed.reshape(4, 1, 2, 8, 2 * MY)
        mixed = jnp.broadcast_to(mixed, (4, 4, 2, 8, 2 * MY)).reshape(32, 8, 2 * MY)
    with jax.named_scope("spread_modes"):
        modes = lax.all_to_all(mixed, column, 0, 0, tiled=True).reshape(MX, 2 * MY)
    with jax.named_scope("pointwise"):
        point = [pointwise(RAW_CUTS[j], image, sibling, cross[j], kron) for j in range(2)]
    modes, point[0], following = lax.optimization_barrier((modes, point[0], following))
    with jax.named_scope("rowback"):
        mode_re, mode_im = modes[:, :MY], modes[:, MY:]
        turned = jnp.concatenate([modes, jnp.concatenate([-mode_im, mode_re], 1)], 0)
        back = jnp.dot(row_tab, turned, preferred_element_type=jnp.float32)
        back = (back * (1.0 / math.sqrt(MX) / math.sqrt(MY))).astype(jnp.bfloat16)
        back = back.reshape(8, rows, 2 * MY)
    with jax.named_scope("swap_back"):
        back = lax.all_to_all(back, group, 0, 0, tiled=True)
    out = most(back, back_cols, bias_rows, *point, soon, following)
    back_tiles = jnp.asarray(np.ascontiguousarray(cols_np[-3 * TILE :].T))
    return rest(back, back_tiles, bias_rows, late, half, end, out)


def solution(mesh):
    fine = Mesh(mesh.devices.reshape(4, 2, 4, 2, 2, 2), ("x", "yh", "zh", "zl", "yl", "core"))
    row, chan = ("x", "yh", "zh", "zl"), ("yl", "core")
    in_specs = (P(chan, row, None), P(None, row, None, chan, None), P(), P(chan))
    return jax.shard_map(
        on_device, mesh=fine, in_specs=in_specs, out_specs=P(chan, row, None), check_vma=False
    )
```

time: 207 us -> 119 us (0.57); the launches traced: 204 us -> 119 us
  waiting for transfers between devices: 107 us -> 32.6 us
  matrix products: 40.9 us -> 9.24 us
  Pallas kernels: 0 us -> 23.2 us
  starting transfers between devices: 33.2 us -> 40.7 us
  local copies, waits for them, and re-layouts: 15.9 us -> 10.2 us
  blocking collectives: 5.43 us -> 0 us
    ppermute x9, waiting for transfers between devices: 76.1 us -> 9.93 us  [the longest x5 7.18 us: send(): return lax.ppermute(src, 'yl', PAIR)]
    dot_general x2, matrix products: 30.5 us -> 0.94 us  [spread(): full = jnp.dot(full, jnp.asarray(wide, jnp.bfloat16))]
    pallas_call x0 -> x5, Pallas kernels: none -> 23.2 us  [the longest x2 7.31 us: pointwise(): pl.pallas_call(pointwise_kernel, grid=(steps,), in_specs=[block(chan, row...]
    all_to_all x4 -> x5, waiting for transfers between devices: 31.3 us -> 22.7 us  [the longest x1 5.99 us: on_device(): part = lax.all_to_all(part, ('yh', 'yl', 'core'), 0, 0, tiled=True)]
    all_gather x1 -> x0, blocking collectives: 5.43 us -> none  [on_device(): zed = lax.all_gather(spectrum, ('yl', 'core'), axis=0, tiled=True)]
    ppermute x9, starting transfers between devices: 4.07 us -> 9.2 us  [the longest x5 6.24 us: send(): return lax.ppermute(src, 'yl', PAIR)]
    convert_element_type x1 -> x0, local copies, waits for them, and re-layouts: 4.31 us -> none  [on_device(): return jax.nn.gelu(total, approximate=False).astype(jnp.bfloat16)]
    unnamed x9 -> x34, local copies, waits for them, and re-layouts: 6.57 us -> 2.88 us
  transfers between devices with their start and end apart: 13 -> 14, of which waited for: 7 -> 9; matrix products, arithmetic and copies ran while one was open for 9% -> 15% of each run, Pallas kernels for 0% -> 17%
where the time goes in v3:
time: 119 us
  starting transfers between devices  40.7 us (34%)
  waiting for transfers between devices  32.6 us (27%)
  Pallas kernels  23.2 us (19%)
  local copies, waits for them, and re-layouts  10.2 us (9%)
  matrix products  9.24 us (8%)
  other arithmetic  2.21 us (2%)
    all_to_all x1, starting transfers between devices, on_device(): part = lax.all_to_all(part, column, 0, 0, tiled=True)  11.2 us
    pallas_call x2, Pallas kernels, pointwise(): pl.pallas_call(pointwise_kernel, grid=(steps,), in_specs=[block(chan, row...  7.31 us
    ppermute x5, waiting for transfers between devices, send(): return lax.ppermute(src, 'yl', PAIR)  7.18 us
    pallas_call x1, Pallas kernels, most(): pl.pallas_call(most_kernel, grid=(cuts[2] + 1,), in_specs=[still(rb), pl....  7.1 us
    dot_general x1, matrix products, on_device(): jnp.dot(image.reshape(chan * rows, width), fwd_cols, preferred_element_ty...  6.61 us
    ppermute x5, starting transfers between devices, send(): return lax.ppermute(src, 'yl', PAIR)  6.24 us
    all_to_all x1, starting transfers between devices, on_device(): modes = lax.all_to_all(mixed, column, 0, 0, tiled=True).reshape(MX, 2 * MY)  6.08 us
    pallas_call x1, Pallas kernels, product(): pl.pallas_call(product_kernel, grid=(tiles,), in_specs=[block(chan, rows,...  6.04 us
  transfers between devices with their start and end apart: 14, of which 9 were waited for; matrix products, arithmetic and copies ran while one was open for 15% of the time, Pallas kernels for 17%

profile of v3, /device:TPU:32, one launch (start us, length us, event | category | flops | bytes accessed | tf_op | source)
XLA Modules:
  0.0 118.5 jit_solution(18016352806220925115)
XLA Ops:
  0.0 1.3 %slice.39 = bf16[8,64,1024]{2,1,0:T(8,128)(2,1)S(1)} slice(bf16[8,64,4096]{2,1,0:T(8,128)(2,1)} %own_ref.5), slice={[0:8], [0:64], [0:1024]} | slice | bytes 2097152 | tf_op jit(solution)/shard_map/slice | solution.py:259
  1.4 1.7 %collective-permute-start = (bf16[8,64,1024]{2,1,0:T(8,128)(2,1)S(1)}, bf16[8,64,1024]{2,1,0:T(8,128)(2,1)}, u32[]{:S(2)}, u32[]{:S(2)}) collective-permute-start(bf16[8,64,1024]{2,1,0:T(8,128)(2,1)S(1)} %slice.39), channel_id=1, source_target_pairs={{0,2},{2,0},{1,3},{3,1},{4,6},{6,4},{5,7},{7,5},{8,10},{10,8},{9,1... | collective-permute-start | bytes 3145736 | tf_op jit(solution)/shard_map/ppermute | solution.py:256
  3.1 6.6 %fusion = bf16[512,512]{0,1:T(8,128)(2,1)} fusion(bf16[512,4096]{1,0:T(8,128)(2,1)} %bitcast.61, bf16[4096,512]{1,0:T(8,128)(2,1)} %constant.117.clone), kind=kOutput, calls=%fused_computation.6 | convolution fusion | flops 2148007936 | bytes 8912896 | tf_op jit(solution)/shard_map/colspec/dot_general | solution.py:272
  9.7 5.8 %all-to-all-start = ((bf16[8,64,512]{2,1,0:T(8,128)(2,1)}), bf16[8,64,512]{2,1,0:T(8,128)(2,1)S(1)}, u32[]{:S(2)}, u32[]{:S(2)}) async-start(bf16[8,64,512]{2,1,0:T(8,128)(2,1)} %bitcast.11), calls=%async_computation | async-start | bytes 1048576 | tf_op jit(solution)/shard_map/swap_rows/all_to_all | solution.py:279
  15.5 2.4 %slice.45 = bf16[8,64,1024]{2,1,0:T(8,128)(2,1)} slice(bf16[8,64,4096]{2,1,0:T(8,128)(2,1)} %own_ref.5), slice={[0:8], [0:64], [1024:2048]} | slice | bytes 2097152 | tf_op jit(solution)/shard_map/slice | solution.py:259
  18.4 1.1 constant_dynamic-slice_fusion
  19.5 5.2 %all-to-all-done = bf16[8,64,512]{2,1,0:T(8,128)(2,1)S(1)} async-done(((bf16[8,64,512]{2,1,0:T(8,128)(2,1)}), bf16[8,64,512]{2,1,0:T(8,128)(2,1)S(1)}, u32[]{:S(2)}, u32[]{:S(2)}) %all-to-all-start) | async-done | bytes 524320 | tf_op jit(solution)/shard_map/swap_rows/all_to_all | solution.py:279
  24.7 2.9 %collective-permute-done.cross_ref = bf16[8,64,1024]{2,1,0:T(8,128)(2,1)} collective-permute-done((bf16[8,64,1024]{2,1,0:T(8,128)(2,1)S(1)}, bf16[8,64,1024]{2,1,0:T(8,128)(2,1)}, u32[]{:S(2)}, u32[]{:S(2)}) %collective-permute-start) | collective-permute-done | bytes 1048608 | tf_op jit(solution)/shard_map/ppermute | solution.py:256
  28.9 11.2 %all-to-all-start.1 = ((bf16[32,8,512]{2,1,0:T(8,128)(2,1)}), bf16[32,8,512]{2,1,0:T(8,128)(2,1)S(1)}, u32[]{:S(2)}, u32[]{:S(2)}) async-start(bf16[32,8,512]{2,1,0:T(8,128)(2,1)} %fusion.10), calls=%async_computation.1 | async-start | bytes 524288 | tf_op jit(solution)/shard_map/swap_modes/all_to_all | solution.py:291
  41.9 6.0 %product.1 = (bf16[8,64,512]{2,1,0:T(8,128)(2,1)}, bf16[8,64,1536]{2,1,0:T(8,128)(2,1)}, bf16[4,64,512]{2,1,0:T(8,128)(2,1)}, bf16[8,64,512]{2,1,0:T(8,128)(2,1)}, bf16[20,64,512]{2,1,0:T(8,128)(2,1)}) custom-call(bf16[8,64,4096]{2,1,0:T(8,128)(2,1)} %own_ref.5, bf16[8,64,4096]{2,1,0:T(8,128)(2,1)} %collective-permute-done.1.sib_ref, ...), custom_call_target="tpu_custom_call" | custom-call | flops 1073741824 | bytes 8388608 | tf_op jit(solution)/shard_map/products/product/pallas_call | solution.py:101
  48.0 3.7 %all-to-all-done.1 = bf16[32,8,512]{2,1,0:T(8,128)(2,1)S(1)} async-done(((bf16[32,8,512]{2,1,0:T(8,128)(2,1)}), bf16[32,8,512]{2,1,0:T(8,128)(2,1)S(1)}, u32[]{:S(2)}, u32[]{:S(2)}) %all-to-all-start.1) | async-done | bytes 262176 | tf_op jit(solution)/shard_map/swap_modes/all_to_all | solution.py:291
  51.8 0.8 broadcast_in_dim.17
  52.6 4.5 %all-to-all-start.2 = ((bf16[64,4,512]{2,1,0:T(4,128)(2,1)}), bf16[64,4,512]{2,1,0:T(4,128)(2,1)S(1)}, u32[]{:S(2)}, u32[]{:S(2)}) async-start(bf16[64,4,512]{2,1,0:T(4,128)(2,1)} %bitcast.17), calls=%async_computation.2 | async-start | bytes 524288 | tf_op jit(solution)/shard_map/gather_chan/all_to_all | solution.py:303
  57.0 2.0 %collective-permute-start.3 = (bf16[4,64,512]{2,1,0:T(8,128)(2,1)}, bf16[4,64,512]{2,1,0:T(8,128)(2,1)S(1)}, u32[]{:S(2)}, u32[]{:S(2)}) collective-permute-start(bf16[4,64,512]{2,1,0:T(8,128)(2,1)} %get-tuple-element.46), channel_id=1, source_target_pairs={{0,2},{2,0},{1,3},{3,1},{4,6},{6,4},{5,7},{7,5},{8,10},{10,8},{9,1... | collective-permute-start | bytes 786440 | tf_op jit(solution)/shard_map/ppermute | solution.py:256
  59.1 6.0 %all-to-all-done.2 = bf16[64,4,512]{2,1,0:T(4,128)(2,1)S(1)} async-done(((bf16[64,4,512]{2,1,0:T(4,128)(2,1)}), bf16[64,4,512]{2,1,0:T(4,128)(2,1)S(1)}, u32[]{:S(2)}, u32[]{:S(2)}) %all-to-all-start.2) | async-done | bytes 262176 | tf_op jit(solution)/shard_map/gather_chan/all_to_all | solution.py:303
  65.9 2.8 %collective-permute-done.3.half_ref = bf16[4,64,512]{2,1,0:T(8,128)(2,1)S(1)} collective-permute-done((bf16[4,64,512]{2,1,0:T(8,128)(2,1)}, bf16[4,64,512]{2,1,0:T(8,128)(2,1)S(1)}, u32[]{:S(2)}, u32[]{:S(2)}) %collective-permute-start.3) | collective-permute-done | bytes 262176 | tf_op jit(solution)/shard_map/ppermute | solution.py:256
  68.7 2.7 %collective-permute-start.4 = (bf16[8,4,512]{2,1,0:T(4,128)(2,1)S(1)}, bf16[8,4,512]{2,1,0:T(4,128)(2,1)S(1)}, u32[]{:S(2)}, u32[]{:S(2)}) collective-permute-start(bf16[8,4,512]{2,1,0:T(4,128)(2,1)S(1)} %pad_maximum_fusion.2), channel_id=1, source_target_pairs={{0,32},{32,0},{1,33},{33,1},{2,34},{34,2},{3,35},{35,3},{4,36},{36... | collective-permute-start | bytes 98312 | tf_op jit(solution)/shard_map/join_halves/ppermute | solution.py:320
  71.4 2.7 %collective-permute-done.4 = bf16[8,4,512]{2,1,0:T(4,128)(2,1)S(1)} collective-permute-done((bf16[8,4,512]{2,1,0:T(4,128)(2,1)S(1)}, bf16[8,4,512]{2,1,0:T(4,128)(2,1)S(1)}, u32[]{:S(2)}, u32[]{:S(2)}) %collective-permute-start.4) | collective-permute-done | bytes 32800 | tf_op jit(solution)/shard_map/join_halves/ppermute | solution.py:320
  75.3 6.1 %all-to-all-start.3 = ((bf16[32,8,512]{2,1,0:T(8,128)(2,1)}), bf16[32,8,512]{2,1,0:T(8,128)(2,1)S(1)}, u32[]{:S(2)}, u32[]{:S(2)}) async-start(bf16[32,8,512]{2,1,0:T(8,128)(2,1)} %bitcast.28), calls=%async_computation.3 | async-start | bytes 524288 | tf_op jit(solution)/shard_map/spread_modes/all_to_all | solution.py:330
  81.4 1.8 %collective-permute-start.7 = (bf16[20,64,512]{2,1,0:T(8,128)(2,1)}, bf16[20,64,512]{2,1,0:T(8,128)(2,1)S(1)}, u32[]{:S(2)}, u32[]{:S(2)}) collective-permute-start(bf16[20,64,512]{2,1,0:T(8,128)(2,1)} %get-tuple-element.58), channel_id=1, source_target_pairs={{0,2},{2,0},{1,3},{3,1},{4,6},{6,4},{5,7},{7,5},{8,10},{10,8},{9,1... | collective-permute-start | bytes 3932168 | tf_op jit(solution)/shard_map/join_halves/ppermute | solution.py:256
  83.2 1.0 copy-done.8
  84.2 3.6 %pointwise.2.first_ref = bf16[8,64,1024]{2,1,0:T(8,128)(2,1)} custom-call(bf16[8,64,4096]{2,1,0:T(8,128)(2,1)} %own_ref.5, bf16[8,64,4096]{2,1,0:T(8,128)(2,1)} %collective-permute-done.1.sib_ref, bf16[8,64,1024]{2,1,0:T(8,128)(2,1)} %collective-permute-done.cross_ref, bf16[8,64,1024]{2,1,0:T(8,128)(2,1)} %copy-done.8, bf16[128,512]{1,0:T(8,128)(2,1)} %copy-done.7), custom_call_target="tpu_custom_call" | custom-call | flops 536870912 | bytes 5242880 | tf_op jit(solution)/shard_map/pointwise/pointwise/pallas_call | solution.py:131
  87.8 4.7 %all-to-all-done.3 = bf16[32,8,512]{2,1,0:T(8,128)(2,1)S(1)} async-done(((bf16[32,8,512]{2,1,0:T(8,128)(2,1)}), bf16[32,8,512]{2,1,0:T(8,128)(2,1)S(1)}, u32[]{:S(2)}, u32[]{:S(2)}) %all-to-all-start.3) | async-done | bytes 262176 | tf_op jit(solution)/shard_map/spread_modes/all_to_all | solution.py:330
  92.5 1.2 %fusion.1 = bf16[512,512]{1,0:T(8,128)(2,1)} fusion(bf16[512,512]{1,0:T(8,128)(2,1)S(1)} %bitcast.64, bf16[256,256]{1,0:T(8,128)(2,1)S(1)} %get-tuple-element.72, bf16[256,256]{1,0:T(8,128)(2,1)S(1)} %get-tuple-element.71, bf16[256,512]{1,0:T(8,128)(2,1)S(1)} %bitcast.67), kind=kOutput, calls=%fused_computation.7 | convolution fusion | flops 270532608 | bytes 1572864 | tf_op jit(solution)/shard_map/rowback/dot_general | solution.py:337
  93.8 4.0 %all-to-all-start.4 = ((bf16[8,64,512]{2,1,0:T(8,128)(2,1)}), bf16[8,64,512]{2,1,0:T(8,128)(2,1)S(1)}, u32[]{:S(2)}, u32[]{:S(2)}) async-start(bf16[8,64,512]{2,1,0:T(8,128)(2,1)} %bitcast.30), calls=%async_computation.4 | async-start | bytes 1048576 | tf_op jit(solution)/shard_map/swap_back/all_to_all | solution.py:341
  98.5 3.7 %pointwise.3.second_ref = bf16[8,64,1024]{2,1,0:T(8,128)(2,1)} custom-call(bf16[8,64,4096]{2,1,0:T(8,128)(2,1)} %own_ref.5, bf16[8,64,4096]{2,1,0:T(8,128)(2,1)} %collective-permute-done.1.sib_ref, bf16[8,64,1024]{2,1,0:T(8,128)(2,1)} %collective-permute-done.2.cross_ref, bf16[8,64,1024]{2,1,0:T(8,128)(2,1)} %collective-permute-done.8.csib_ref, ...), custom_call_target="tpu_custom_call" | custom-call | flops 536870912 | bytes 5242880 | tf_op jit(solution)/shard_map/pointwise/pointwise/pallas_call | solution.py:131
  102.2 3.1 %all-to-all-done.4.rb_ref = bf16[8,64,512]{2,1,0:T(8,128)(2,1)S(1)} async-done(((bf16[8,64,512]{2,1,0:T(8,128)(2,1)}), bf16[8,64,512]{2,1,0:T(8,128)(2,1)S(1)}, u32[]{:S(2)}, u32[]{:S(2)}) %all-to-all-start.4) | async-done | bytes 524320 | tf_op jit(solution)/shard_map/swap_back/all_to_all | solution.py:341
  105.3 0.8 copy-done
  106.1 7.1 %most.1.so_far_ref = bf16[8,64,4096]{2,1,0:T(8,128)(2,1)} custom-call(bf16[8,64,512]{2,1,0:T(8,128)(2,1)} %copy-done, bf16[512,4096]{1,0:T(8,128)(2,1)} %constant.118.clone.back_ref, f32[128,1]{1,0:T(8,128)} %copy.33.bias_ref, bf16[8,64,1024]{2,1,0:T(8,128)(2,1)} %pointwise.2.first_ref, bf16[8,64,1024]{2,1,0:T(8,128)(2,1)} %pointwise.3.second_ref, ...), custom_call_target="tpu_custom_call" | custom-call | flops 1 | bytes 1 | tf_op jit(solution)/shard_map/most/pallas_call | solution.py:194
  113.2 1.5 %collective-permute-done.7.end_ref = bf16[20,64,512]{2,1,0:T(8,128)(2,1)S(1)} collective-permute-done((bf16[20,64,512]{2,1,0:T(8,128)(2,1)}, bf16[20,64,512]{2,1,0:T(8,128)(2,1)S(1)}, u32[]{:S(2)}, u32[]{:S(2)}) %collective-permute-start.7) | collective-permute-done | bytes 1310752 | tf_op jit(solution)/shard_map/join_halves/ppermute | solution.py:256
  114.8 1.0 copy-done.1
  115.8 2.7 %rest.1 = bf16[8,64,4096]{2,1,0:T(8,128)(2,1)} custom-call(bf16[8,64,512]{2,1,0:T(8,128)(2,1)S(1)} %copy-done.1, bf16[512,1536]{1,0:T(8,128)(2,1)S(1)} %copy-done.2, f32[128,1]{1,0:T(8,128)S(1)} %copy-done.4, bf16[8,64,1536]{2,1,0:T(8,128)(2,1)S(1)} %copy-done.3, bf16[4,64,512]{2,1,0:T(8,128)(2,1)S(1)} %copy-done.6, ...), custom_call_target="tpu_custom_call", output_to_operand_aliasing={{}: (6, {})} | custom-call | flops 1 | bytes 1 | tf_op jit(solution)/shard_map/rest/pallas_call | solution.py:231
  (66 shorter events, 6.6 us)
Async XLA Ops:
  1.3 40.6 %collective-permute-start.1 = (bf16[8,64,4096]{2,1,0:T(8,128)(2,1)}, bf16[8,64,4096]{2,1,0:T(8,128)(2,1)}, u32[]{:S(2)}, u32[]{:S(2)}) collective-permute-start(bf16[8,64,4096]{2,1,0:T(8,128)(2,1)} %own_ref.5), channel_id=1, source_target_pairs={{0,1},{1,0},{2,3},{3,2},{4,5},{5,4},{6,7},{7,6},{8,9},{9,8},{10,11... | collective-permute-start | bytes 12582920 | tf_op jit(solution)/shard_map/ppermute | solution.py:263
  1.4 26.2 %collective-permute-start = (bf16[8,64,1024]{2,1,0:T(8,128)(2,1)S(1)}, bf16[8,64,1024]{2,1,0:T(8,128)(2,1)}, u32[]{:S(2)}, u32[]{:S(2)}) collective-permute-start(bf16[8,64,1024]{2,1,0:T(8,128)(2,1)S(1)} %slice.39), channel_id=1, source_target_pairs={{0,2},{2,0},{1,3},{3,1},{4,6},{6,4},{5,7},{7,5},{8,10},{10,8},{9,1... | collective-permute-start | bytes 3145736 | tf_op jit(solution)/shard_map/ppermute | solution.py:256
  3.1 15.2 %copy-start.14 = (bf16[32,32]{1,0:T(8,128)(2,1)S(1)}, bf16[32,32]{1,0:T(8,128)(2,1)}, u32[]{:S(2)}) copy-start(bf16[32,32]{1,0:T(8,128)(2,1)} %param.16) | copy-start | bytes 6148
  9.7 15.0 %all-to-all-start = ((bf16[8,64,512]{2,1,0:T(8,128)(2,1)}), bf16[8,64,512]{2,1,0:T(8,128)(2,1)S(1)}, u32[]{:S(2)}, u32[]{:S(2)}) async-start(bf16[8,64,512]{2,1,0:T(8,128)(2,1)} %bitcast.11), calls=%async_computation | async-start | bytes 1048576 | tf_op jit(solution)/shard_map/swap_rows/all_to_all | solution.py:279
  15.5 24.6 %copy-start.10 = (bf16[128,512]{1,0:T(8,128)(2,1)S(1)}, bf16[128,512]{1,0:T(8,128)(2,1)}, u32[]{:S(2)}) copy-start(bf16[128,512]{1,0:T(8,128)(2,1)} %constant.122.clone) | copy-start | bytes 393220
  15.5 24.6 %copy-start.11 = (bf16[128,8]{1,0:T(8,128)(2,1)S(1)}, bf16[128,8]{1,0:T(8,128)(2,1)}, u32[]{:S(2)}) copy-start(bf16[128,8]{1,0:T(8,128)(2,1)} %constant.120.clone) | copy-start | bytes 6148
  15.5 24.6 %copy-start.13 = (bf16[32,512]{1,0:T(8,128)(2,1)S(1)}, bf16[32,512]{1,0:T(8,128)(2,1)}, u32[]{:S(2)}) copy-start(bf16[32,512]{1,0:T(8,128)(2,1)} %constant.121.clone) | copy-start | bytes 98308
  15.5 25.1 %copy-start.16 = (f32[8]{0:T(128)S(1)}, f32[8]{0:T(128)}, u32[]{:S(2)}) copy-start(f32[8]{0:T(128)} %param.17) | copy-start | bytes 100
  15.5 25.3 %copy-start.12 = (bf16[128,256]{1,0:T(8,128)(2,1)S(1)}, bf16[128,256]{1,0:T(8,128)(2,1)}, u32[]{:S(2)}) copy-start(bf16[128,256]{1,0:T(8,128)(2,1)} %constant.124.clone) | copy-start | bytes 196612
  15.5 25.3 %copy-start.15 = (bf16[16,256]{1,0:T(8,128)(2,1)S(1)}, bf16[16,256]{1,0:T(8,128)(2,1)}, u32[]{:S(2)}) copy-start(bf16[16,256]{1,0:T(8,128)(2,1)} %constant.123.clone) | copy-start | bytes 24580
  17.9 41.2 %collective-permute-start.2 = (bf16[8,64,1024]{2,1,0:T(8,128)(2,1)}, bf16[8,64,1024]{2,1,0:T(8,128)(2,1)}, u32[]{:S(2)}, u32[]{:S(2)}) collective-permute-start(bf16[8,64,1024]{2,1,0:T(8,128)(2,1)} %slice.45), channel_id=1, source_target_pairs={{0,2},{2,0},{1,3},{3,1},{4,6},{6,4},{5,7},{7,5},{8,10},{10,8},{9,1... | collective-permute-start | bytes 3145736 | tf_op jit(solution)/shard_map/ppermute | solution.py:256
  28.9 22.8 %all-to-all-start.1 = ((bf16[32,8,512]{2,1,0:T(8,128)(2,1)}), bf16[32,8,512]{2,1,0:T(8,128)(2,1)S(1)}, u32[]{:S(2)}, u32[]{:S(2)}) async-start(bf16[32,8,512]{2,1,0:T(8,128)(2,1)} %fusion.10), calls=%async_computation.1 | async-start | bytes 524288 | tf_op jit(solution)/shard_map/swap_modes/all_to_all | solution.py:291
  40.6 7.4 %copy-start.7 = (bf16[128,512]{1,0:T(8,128)(2,1)}, bf16[128,512]{1,0:T(8,128)(2,1)S(1)}, u32[]{:S(2)}) copy-start(bf16[128,512]{1,0:T(8,128)(2,1)S(1)} %convolution_multiply_fusion.2.kron_ref) | copy-start | bytes 393220
  41.9 23.5 %copy-start.9 = (bf16[2,4,32,8,256]{4,3,2,1,0:T(8,128)(2,1)S(1)}, bf16[2,4,32,8,256]{4,3,2,1,0:T(8,128)(2,1)}, u32[]{:S(2)}) copy-start(bf16[2,4,32,8,256]{4,3,2,1,0:T(8,128)(2,1)} %param.15) | copy-start | bytes 3145732
  52.6 12.5 %all-to-all-start.2 = ((bf16[64,4,512]{2,1,0:T(4,128)(2,1)}), bf16[64,4,512]{2,1,0:T(4,128)(2,1)S(1)}, u32[]{:S(2)}, u32[]{:S(2)}) async-start(bf16[64,4,512]{2,1,0:T(4,128)(2,1)} %bitcast.17), calls=%async_computation.2 | async-start | bytes 524288 | tf_op jit(solution)/shard_map/gather_chan/all_to_all | solution.py:303
  57.0 11.7 %collective-permute-start.3 = (bf16[4,64,512]{2,1,0:T(8,128)(2,1)}, bf16[4,64,512]{2,1,0:T(8,128)(2,1)S(1)}, u32[]{:S(2)}, u32[]{:S(2)}) collective-permute-start(bf16[4,64,512]{2,1,0:T(8,128)(2,1)} %get-tuple-element.46), channel_id=1, source_target_pairs={{0,2},{2,0},{1,3},{3,1},{4,6},{6,4},{5,7},{7,5},{8,10},{10,8},{9,1... | collective-permute-start | bytes 786440 | tf_op jit(solution)/shard_map/ppermute | solution.py:256
  65.3 17.9 %collective-permute-start.5 = (bf16[8,64,1024]{2,1,0:T(8,128)(2,1)}, bf16[8,64,1024]{2,1,0:T(8,128)(2,1)S(1)}, u32[]{:S(2)}, u32[]{:S(2)}) collective-permute-start(bf16[8,64,1024]{2,1,0:T(8,128)(2,1)} %collective-permute-done.cross_ref), channel_id=1, source_target_pairs={{0,1},{1,0},{2,3},{3,2},{4,5},{5,4},{6,7},{7,6},{8,9},{9,8},{10,11... | collective-permute-start | bytes 3145736 | tf_op jit(solution)/shard_map/pointwise/ppermute | solution.py:146
  68.7 19.1 %copy-start.5 = (bf16[4,64,512]{2,1,0:T(8,128)(2,1)}, bf16[4,64,512]{2,1,0:T(8,128)(2,1)S(1)}, u32[]{:S(2)}) copy-start(bf16[4,64,512]{2,1,0:T(8,128)(2,1)S(1)} %collective-permute-done.3.half_ref) | copy-start | bytes 786436
  68.7 5.4 %collective-permute-start.4 = (bf16[8,4,512]{2,1,0:T(4,128)(2,1)S(1)}, bf16[8,4,512]{2,1,0:T(4,128)(2,1)S(1)}, u32[]{:S(2)}, u32[]{:S(2)}) collective-permute-start(bf16[8,4,512]{2,1,0:T(4,128)(2,1)S(1)} %pad_maximum_fusion.2), channel_id=1, source_target_pairs={{0,32},{32,0},{1,33},{33,1},{2,34},{34,2},{3,35},{35,3},{4,36},{36... | collective-permute-start | bytes 98312 | tf_op jit(solution)/shard_map/join_halves/ppermute | solution.py:320
  74.1 18.4 %collective-permute-start.6 = (bf16[8,64,512]{2,1,0:T(8,128)(2,1)}, bf16[8,64,512]{2,1,0:T(8,128)(2,1)}, u32[]{:S(2)}, u32[]{:S(2)}) collective-permute-start(bf16[8,64,512]{2,1,0:T(8,128)(2,1)} %get-tuple-element.53), channel_id=1, source_target_pairs={{0,2},{2,0},{1,3},{3,1},{4,6},{6,4},{5,7},{7,5},{8,10},{10,8},{9,1... | collective-permute-start | bytes 1572872 | tf_op jit(solution)/shard_map/join_halves/ppermute | solution.py:256
  75.3 17.2 %all-to-all-start.3 = ((bf16[32,8,512]{2,1,0:T(8,128)(2,1)}), bf16[32,8,512]{2,1,0:T(8,128)(2,1)S(1)}, u32[]{:S(2)}, u32[]{:S(2)}) async-start(bf16[32,8,512]{2,1,0:T(8,128)(2,1)} %bitcast.28), calls=%async_computation.3 | async-start | bytes 524288 | tf_op jit(solution)/shard_map/spread_modes/all_to_all | solution.py:330
  81.3 17.2 %collective-permute-start.8 = (bf16[8,64,1024]{2,1,0:T(8,128)(2,1)}, bf16[8,64,1024]{2,1,0:T(8,128)(2,1)}, u32[]{:S(2)}, u32[]{:S(2)}) collective-permute-start(bf16[8,64,1024]{2,1,0:T(8,128)(2,1)} %collective-permute-done.2.cross_ref), channel_id=1, source_target_pairs={{0,1},{1,0},{2,3},{3,2},{4,5},{5,4},{6,7},{7,6},{8,9},{9,8},{10,11... | collective-permute-start | bytes 3145736 | tf_op jit(solution)/shard_map/pointwise/ppermute | solution.py:146
  81.4 33.3 %collective-permute-start.7 = (bf16[20,64,512]{2,1,0:T(8,128)(2,1)}, bf16[20,64,512]{2,1,0:T(8,128)(2,1)S(1)}, u32[]{:S(2)}, u32[]{:S(2)}) collective-permute-start(bf16[20,64,512]{2,1,0:T(8,128)(2,1)} %get-tuple-element.58), channel_id=1, source_target_pairs={{0,2},{2,0},{1,3},{3,1},{4,6},{6,4},{5,7},{7,5},{8,10},{10,8},{9,1... | collective-permute-start | bytes 3932168 | tf_op jit(solution)/shard_map/join_halves/ppermute | solution.py:256
  83.2 1.0 copy-start.8
  93.8 11.6 %all-to-all-start.4 = ((bf16[8,64,512]{2,1,0:T(8,128)(2,1)}), bf16[8,64,512]{2,1,0:T(8,128)(2,1)S(1)}, u32[]{:S(2)}, u32[]{:S(2)}) async-start(bf16[8,64,512]{2,1,0:T(8,128)(2,1)} %bitcast.30), calls=%async_computation.4 | async-start | bytes 1048576 | tf_op jit(solution)/shard_map/swap_back/all_to_all | solution.py:341
  102.2 12.5 %copy-start.2 = (bf16[512,1536]{1,0:T(8,128)(2,1)S(1)}, bf16[512,1536]{1,0:T(8,128)(2,1)}, u32[]{:S(2)}) copy-start(bf16[512,1536]{1,0:T(8,128)(2,1)} %constant.125.clone.back_ref) | copy-start | bytes 4718596
  102.2 12.5 %copy-start.4 = (f32[128,1]{1,0:T(8,128)S(1)}, f32[128,1]{1,0:T(8,128)}, u32[]{:S(2)}) copy-start(f32[128,1]{1,0:T(8,128)} %copy.33.bias_ref) | copy-start | bytes 1540
  105.3 0.8 copy-start
  106.1 8.6 %copy-start.3 = (bf16[8,64,1536]{2,1,0:T(8,128)(2,1)S(1)}, bf16[8,64,1536]{2,1,0:T(8,128)(2,1)}, u32[]{:S(2)}) copy-start(bf16[8,64,1536]{2,1,0:T(8,128)(2,1)} %get-tuple-element.56.late_ref) | copy-start | bytes 4718596
  106.1 8.6 %copy-start.6 = (bf16[4,64,512]{2,1,0:T(8,128)(2,1)S(1)}, bf16[4,64,512]{2,1,0:T(8,128)(2,1)}, u32[]{:S(2)}) copy-start(bf16[4,64,512]{2,1,0:T(8,128)(2,1)} %copy-done.5) | copy-start | bytes 786436
  114.7 1.0 copy-start.1

commit v4 on v3

--- a/solution.py
+++ b/solution.py
@@ -71,9 +71,9 @@
     for t, (mine_ref, place, theirs) in enumerate(
         (
             (soon_ref, 0, ((next_ref, 0, 8),)),
-            (late_ref, 0, ((half_ref, 0, 4), (end_ref, 0, 4))),
-            (late_ref, 1, ((end_ref, 4, 8),)),
-            (late_ref, 2, ((end_ref, 12, 8),)),
+            (late_ref, 0, ((half_ref, 0, 3), (end_ref, 0, 5))),
+            (late_ref, 1, ((end_ref, 5, 8),)),
+            (late_ref, 2, ((end_ref, 13, 8),)),
         )
     ):
 
@@ -97,7 +97,7 @@
 def product(image, sibling, kron):
     chan, rows, width = image.shape
     first, tiles = RAW // TILE, (width - RAW) // TILE
-    sizes = [(chan, TILE), (chan, 3 * TILE), (4, TILE), (8, TILE), (20, TILE)]
+    sizes = [(chan, TILE), (chan, 3 * TILE), (3, TILE), (8, TILE), (21, TILE)]
     return pl.pallas_call(
         product_kernel,
         grid=(tiles,),
@@ -195,7 +195,7 @@
         most_kernel,
         grid=(cuts[2] + 1,),
         in_specs=[
-            still(rb),
+            pl.BlockSpec(memory_space=pltpu.VMEM),
             pl.BlockSpec((2 * MY, TILE), lambda w: (0, w)),
             still(bias_rows),
             block(chan, rows, 0, cuts[1]),
@@ -205,7 +205,7 @@
         ],
         out_specs=block(chan, rows),
         out_shape=jax.ShapeDtypeStruct((chan, rows, width), jnp.bfloat16),
-        compiler_params=pltpu.CompilerParams(vmem_limit_bytes=VMEM),
+        compiler_params=pltpu.CompilerParams(vmem_limit_bytes=56 * 2**20),
         cost_estimate=pl.CostEstimate(flops=1, bytes_accessed=1, transcendentals=0),
         name="most",
     )(rb, back_cols, bias_rows, first, second, soon, following)
@@ -213,9 +213,9 @@
 
 def rest_kernel(rb_ref, back_ref, bias_ref, late_ref, half_ref, end_ref, so_far_ref, out_ref):
     others = (
-        [(half_ref, 0, 4, 0), (end_ref, 0, 4, 0)],
-        [(end_ref, 4, 8, 0)],
-        [(end_ref, 12, 8, 0)],
+        [(half_ref, 0, 3, 0), (end_ref, 0, 5, 0)],
+        [(end_ref, 5, 8, 0)],
+        [(end_ref, 13, 8, 0)],
     )
     for t, other in enumerate(others):
 

time: 119 us -> 119 us (level)
  no operation moved by 1% of the time
where the time goes in v4:
time: 119 us
  starting transfers between devices  40.8 us (34%)
  waiting for transfers between devices  32.6 us (27%)
  Pallas kernels  23.2 us (19%)
  local copies, waits for them, and re-layouts  10.2 us (9%)
  matrix products  9.24 us (8%)
  other arithmetic  2.21 us (2%)
    all_to_all x1, starting transfers between devices, on_device(): part = lax.all_to_all(part, column, 0, 0, tiled=True)  11.2 us
    pallas_call x2, Pallas kernels, pointwise(): pl.pallas_call(pointwise_kernel, grid=(steps,), in_specs=[block(chan, row...  7.28 us
    ppermute x5, waiting for transfers between devices, send(): return lax.ppermute(src, 'yl', PAIR)  7.13 us
    pallas_call x1, Pallas kernels, most(): pl.pallas_call(most_kernel, grid=(cuts[2] + 1,), in_specs=[pl.BlockSpec(m...  7.1 us
    dot_general x1, matrix products, on_device(): jnp.dot(image.reshape(chan * rows, width), fwd_cols, preferred_element_ty...  6.61 us
    ppermute x5, starting transfers between devices, send(): return lax.ppermute(src, 'yl', PAIR)  6.24 us
    all_to_all x1, starting transfers between devices, on_device(): modes = lax.all_to_all(mixed, column, 0, 0, tiled=True).reshape(MX, 2 * MY)  6.13 us
    pallas_call x1, Pallas kernels, product(): pl.pallas_call(product_kernel, grid=(tiles,), in_specs=[block(chan, rows,...  6.1 us
  transfers between devices with their start and end apart: 14, of which 9 were waited for; matrix products, arithmetic and copies ran while one was open for 15% of the time, Pallas kernels for 17%

profile of v4, /device:TPU:32, one launch (start us, length us, event | category | flops | bytes accessed | tf_op | source)
XLA Modules:
  0.0 118.5 jit_solution(12796919576943939200)
XLA Ops:
  0.0 1.3 %slice.39 = bf16[8,64,1024]{2,1,0:T(8,128)(2,1)S(1)} slice(bf16[8,64,4096]{2,1,0:T(8,128)(2,1)} %own_ref.5), slice={[0:8], [0:64], [0:1024]} | slice | bytes 2097152 | tf_op jit(solution)/shard_map/slice | solution.py:259
  1.4 1.7 %collective-permute-start = (bf16[8,64,1024]{2,1,0:T(8,128)(2,1)S(1)}, bf16[8,64,1024]{2,1,0:T(8,128)(2,1)}, u32[]{:S(2)}, u32[]{:S(2)}) collective-permute-start(bf16[8,64,1024]{2,1,0:T(8,128)(2,1)S(1)} %slice.39), channel_id=1, source_target_pairs={{0,2},{2,0},{1,3},{3,1},{4,6},{6,4},{5,7},{7,5},{8,10},{10,8},{9,1... | collective-permute-start | bytes 3145736 | tf_op jit(solution)/shard_map/ppermute | solution.py:256
  3.1 6.6 %fusion = bf16[512,512]{0,1:T(8,128)(2,1)} fusion(bf16[512,4096]{1,0:T(8,128)(2,1)} %bitcast.61, bf16[4096,512]{1,0:T(8,128)(2,1)} %constant.117.clone), kind=kOutput, calls=%fused_computation.6 | convolution fusion | flops 2148007936 | bytes 8912896 | tf_op jit(solution)/shard_map/colspec/dot_general | solution.py:272
  9.7 5.8 %all-to-all-start = ((bf16[8,64,512]{2,1,0:T(8,128)(2,1)}), bf16[8,64,512]{2,1,0:T(8,128)(2,1)S(1)}, u32[]{:S(2)}, u32[]{:S(2)}) async-start(bf16[8,64,512]{2,1,0:T(8,128)(2,1)} %bitcast.11), calls=%async_computation | async-start | bytes 1048576 | tf_op jit(solution)/shard_map/swap_rows/all_to_all | solution.py:279
  15.5 2.4 %slice.45 = bf16[8,64,1024]{2,1,0:T(8,128)(2,1)} slice(bf16[8,64,4096]{2,1,0:T(8,128)(2,1)} %own_ref.5), slice={[0:8], [0:64], [1024:2048]} | slice | bytes 2097152 | tf_op jit(solution)/shard_map/slice | solution.py:259
  18.4 1.1 constant_dynamic-slice_fusion
  19.5 5.2 %all-to-all-done = bf16[8,64,512]{2,1,0:T(8,128)(2,1)S(1)} async-done(((bf16[8,64,512]{2,1,0:T(8,128)(2,1)}), bf16[8,64,512]{2,1,0:T(8,128)(2,1)S(1)}, u32[]{:S(2)}, u32[]{:S(2)}) %all-to-all-start) | async-done | bytes 524320 | tf_op jit(solution)/shard_map/swap_rows/all_to_all | solution.py:279
  24.7 2.9 %collective-permute-done.cross_ref = bf16[8,64,1024]{2,1,0:T(8,128)(2,1)} collective-permute-done((bf16[8,64,1024]{2,1,0:T(8,128)(2,1)S(1)}, bf16[8,64,1024]{2,1,0:T(8,128)(2,1)}, u32[]{:S(2)}, u32[]{:S(2)}) %collective-permute-start) | collective-permute-done | bytes 1048608 | tf_op jit(solution)/shard_map/ppermute | solution.py:256
  28.9 11.2 %all-to-all-start.1 = ((bf16[32,8,512]{2,1,0:T(8,128)(2,1)}), bf16[32,8,512]{2,1,0:T(8,128)(2,1)S(1)}, u32[]{:S(2)}, u32[]{:S(2)}) async-start(bf16[32,8,512]{2,1,0:T(8,128)(2,1)} %fusion.10), calls=%async_computation.1 | async-start | bytes 524288 | tf_op jit(solution)/shard_map/swap_modes/all_to_all | solution.py:291
  41.9 6.1 %product.1 = (bf16[8,64,512]{2,1,0:T(8,128)(2,1)}, bf16[8,64,1536]{2,1,0:T(8,128)(2,1)}, bf16[3,64,512]{2,1,0:T(8,128)(2,1)}, bf16[8,64,512]{2,1,0:T(8,128)(2,1)}, bf16[21,64,512]{2,1,0:T(8,128)(2,1)}) custom-call(bf16[8,64,4096]{2,1,0:T(8,128)(2,1)} %own_ref.5, bf16[8,64,4096]{2,1,0:T(8,128)(2,1)} %collective-permute-done.1.sib_ref, ...), custom_call_target="tpu_custom_call" | custom-call | flops 1073741824 | bytes 8388608 | tf_op jit(solution)/shard_map/products/product/pallas_call | solution.py:101
  48.0 3.7 %all-to-all-done.1 = bf16[32,8,512]{2,1,0:T(8,128)(2,1)S(1)} async-done(((bf16[32,8,512]{2,1,0:T(8,128)(2,1)}), bf16[32,8,512]{2,1,0:T(8,128)(2,1)S(1)}, u32[]{:S(2)}, u32[]{:S(2)}) %all-to-all-start.1) | async-done | bytes 262176 | tf_op jit(solution)/shard_map/swap_modes/all_to_all | solution.py:291
  51.8 0.8 broadcast_in_dim.17
  52.6 4.5 %all-to-all-start.2 = ((bf16[64,4,512]{2,1,0:T(4,128)(2,1)}), bf16[64,4,512]{2,1,0:T(4,128)(2,1)S(1)}, u32[]{:S(2)}, u32[]{:S(2)}) async-start(bf16[64,4,512]{2,1,0:T(4,128)(2,1)} %bitcast.17), calls=%async_computation.2 | async-start | bytes 524288 | tf_op jit(solution)/shard_map/gather_chan/all_to_all | solution.py:303
  57.0 2.0 %collective-permute-start.3 = (bf16[3,64,512]{2,1,0:T(8,128)(2,1)}, bf16[3,64,512]{2,1,0:T(8,128)(2,1)S(1)}, u32[]{:S(2)}, u32[]{:S(2)}) collective-permute-start(bf16[3,64,512]{2,1,0:T(8,128)(2,1)} %get-tuple-element.46), channel_id=1, source_target_pairs={{0,2},{2,0},{1,3},{3,1},{4,6},{6,4},{5,7},{7,5},{8,10},{10,8},{9,1... | collective-permute-start | bytes 589832 | tf_op jit(solution)/shard_map/ppermute | solution.py:256
  59.1 6.0 %all-to-all-done.2 = bf16[64,4,512]{2,1,0:T(4,128)(2,1)S(1)} async-done(((bf16[64,4,512]{2,1,0:T(4,128)(2,1)}), bf16[64,4,512]{2,1,0:T(4,128)(2,1)S(1)}, u32[]{:S(2)}, u32[]{:S(2)}) %all-to-all-start.2) | async-done | bytes 262176 | tf_op jit(solution)/shard_map/gather_chan/all_to_all | solution.py:303
  65.9 1.4 %collective-permute-done.3.half_ref = bf16[3,64,512]{2,1,0:T(8,128)(2,1)S(1)} collective-permute-done((bf16[3,64,512]{2,1,0:T(8,128)(2,1)}, bf16[3,64,512]{2,1,0:T(8,128)(2,1)S(1)}, u32[]{:S(2)}, u32[]{:S(2)}) %collective-permute-start.3) | collective-permute-done | bytes 196640 | tf_op jit(solution)/shard_map/ppermute | solution.py:256
  67.3 2.7 %collective-permute-start.4 = (bf16[8,4,512]{2,1,0:T(4,128)(2,1)S(1)}, bf16[8,4,512]{2,1,0:T(4,128)(2,1)S(1)}, u32[]{:S(2)}, u32[]{:S(2)}) collective-permute-start(bf16[8,4,512]{2,1,0:T(4,128)(2,1)S(1)} %pad_maximum_fusion.2), channel_id=1, source_target_pairs={{0,32},{32,0},{1,33},{33,1},{2,34},{34,2},{3,35},{35,3},{4,36},{36... | collective-permute-start | bytes 98312 | tf_op jit(solution)/shard_map/join_halves/ppermute | solution.py:320
  70.0 2.7 %collective-permute-done.4 = bf16[8,4,512]{2,1,0:T(4,128)(2,1)S(1)} collective-permute-done((bf16[8,4,512]{2,1,0:T(4,128)(2,1)S(1)}, bf16[8,4,512]{2,1,0:T(4,128)(2,1)S(1)}, u32[]{:S(2)}, u32[]{:S(2)}) %collective-permute-start.4) | collective-permute-done | bytes 32800 | tf_op jit(solution)/shard_map/join_halves/ppermute | solution.py:320
  73.9 6.1 %all-to-all-start.3 = ((bf16[32,8,512]{2,1,0:T(8,128)(2,1)}), bf16[32,8,512]{2,1,0:T(8,128)(2,1)S(1)}, u32[]{:S(2)}, u32[]{:S(2)}) async-start(bf16[32,8,512]{2,1,0:T(8,128)(2,1)} %bitcast.28), calls=%async_computation.3 | async-start | bytes 524288 | tf_op jit(solution)/shard_map/spread_modes/all_to_all | solution.py:330
  80.1 1.8 %collective-permute-start.7 = (bf16[21,64,512]{2,1,0:T(8,128)(2,1)}, bf16[21,64,512]{2,1,0:T(8,128)(2,1)S(1)}, u32[]{:S(2)}, u32[]{:S(2)}) collective-permute-start(bf16[21,64,512]{2,1,0:T(8,128)(2,1)} %get-tuple-element.58), channel_id=1, source_target_pairs={{0,2},{2,0},{1,3},{3,1},{4,6},{6,4},{5,7},{7,5},{8,10},{10,8},{9,1... | collective-permute-start | bytes 4128776 | tf_op jit(solution)/shard_map/join_halves/ppermute | solution.py:256
  81.9 1.0 copy-done.8
  82.8 3.6 %pointwise.2.first_ref = bf16[8,64,1024]{2,1,0:T(8,128)(2,1)} custom-call(bf16[8,64,4096]{2,1,0:T(8,128)(2,1)} %own_ref.5, bf16[8,64,4096]{2,1,0:T(8,128)(2,1)} %collective-permute-done.1.sib_ref, bf16[8,64,1024]{2,1,0:T(8,128)(2,1)} %collective-permute-done.cross_ref, bf16[8,64,1024]{2,1,0:T(8,128)(2,1)} %copy-done.8, bf16[128,512]{1,0:T(8,128)(2,1)} %copy-done.7), custom_call_target="tpu_custom_call" | custom-call | flops 536870912 | bytes 5242880 | tf_op jit(solution)/shard_map/pointwise/pointwise/pallas_call | solution.py:131
  86.4 4.7 %all-to-all-done.3 = bf16[32,8,512]{2,1,0:T(8,128)(2,1)S(1)} async-done(((bf16[32,8,512]{2,1,0:T(8,128)(2,1)}), bf16[32,8,512]{2,1,0:T(8,128)(2,1)S(1)}, u32[]{:S(2)}, u32[]{:S(2)}) %all-to-all-start.3) | async-done | bytes 262176 | tf_op jit(solution)/shard_map/spread_modes/all_to_all | solution.py:330
  91.2 1.2 %fusion.1 = bf16[512,512]{1,0:T(8,128)(2,1)} fusion(bf16[512,512]{1,0:T(8,128)(2,1)S(1)} %bitcast.64, bf16[256,256]{1,0:T(8,128)(2,1)S(1)} %get-tuple-element.72, bf16[256,256]{1,0:T(8,128)(2,1)S(1)} %get-tuple-element.71, bf16[256,512]{1,0:T(8,128)(2,1)S(1)} %bitcast.67), kind=kOutput, calls=%fused_computation.7 | convolution fusion | flops 270532608 | bytes 1572864 | tf_op jit(solution)/shard_map/rowback/dot_general | solution.py:337
  92.4 4.0 %all-to-all-start.4 = ((bf16[8,64,512]{2,1,0:T(8,128)(2,1)}), bf16[8,64,512]{2,1,0:T(8,128)(2,1)S(1)}, u32[]{:S(2)}, u32[]{:S(2)}) async-start(bf16[8,64,512]{2,1,0:T(8,128)(2,1)} %bitcast.30), calls=%async_computation.4 | async-start | bytes 1048576 | tf_op jit(solution)/shard_map/swap_back/all_to_all | solution.py:341
  97.2 3.7 %pointwise.3.second_ref = bf16[8,64,1024]{2,1,0:T(8,128)(2,1)} custom-call(bf16[8,64,4096]{2,1,0:T(8,128)(2,1)} %own_ref.5, bf16[8,64,4096]{2,1,0:T(8,128)(2,1)} %collective-permute-done.1.sib_ref, bf16[8,64,1024]{2,1,0:T(8,128)(2,1)} %collective-permute-done.2.cross_ref, bf16[8,64,1024]{2,1,0:T(8,128)(2,1)} %collective-permute-done.8.csib_ref, ...), custom_call_target="tpu_custom_call" | custom-call | flops 536870912 | bytes 5242880 | tf_op jit(solution)/shard_map/pointwise/pointwise/pallas_call | solution.py:131
  100.9 3.1 %all-to-all-done.4.rb_ref = bf16[8,64,512]{2,1,0:T(8,128)(2,1)S(1)} async-done(((bf16[8,64,512]{2,1,0:T(8,128)(2,1)}), bf16[8,64,512]{2,1,0:T(8,128)(2,1)S(1)}, u32[]{:S(2)}, u32[]{:S(2)}) %all-to-all-start.4) | async-done | bytes 524320 | tf_op jit(solution)/shard_map/swap_back/all_to_all | solution.py:341
  104.0 0.8 copy-done
  104.8 7.1 %most.1.so_far_ref = bf16[8,64,4096]{2,1,0:T(8,128)(2,1)} custom-call(bf16[8,64,512]{2,1,0:T(8,128)(2,1)} %copy-done, bf16[512,4096]{1,0:T(8,128)(2,1)} %constant.118.clone.back_ref, f32[128,1]{1,0:T(8,128)} %copy.33.bias_ref, bf16[8,64,1024]{2,1,0:T(8,128)(2,1)} %pointwise.2.first_ref, bf16[8,64,1024]{2,1,0:T(8,128)(2,1)} %pointwise.3.second_ref, ...), custom_call_target="tpu_custom_call" | custom-call | flops 1 | bytes 1 | tf_op jit(solution)/shard_map/most/pallas_call | solution.py:194
  111.9 2.8 %collective-permute-done.7.end_ref = bf16[21,64,512]{2,1,0:T(8,128)(2,1)S(1)} collective-permute-done((bf16[21,64,512]{2,1,0:T(8,128)(2,1)}, bf16[21,64,512]{2,1,0:T(8,128)(2,1)S(1)}, u32[]{:S(2)}, u32[]{:S(2)}) %collective-permute-start.7) | collective-permute-done | bytes 1376288 | tf_op jit(solution)/shard_map/join_halves/ppermute | solution.py:256
  114.8 1.0 copy-done.1
  115.8 2.7 %rest.1 = bf16[8,64,4096]{2,1,0:T(8,128)(2,1)} custom-call(bf16[8,64,512]{2,1,0:T(8,128)(2,1)S(1)} %copy-done.1, bf16[512,1536]{1,0:T(8,128)(2,1)S(1)} %copy-done.2, f32[128,1]{1,0:T(8,128)S(1)} %copy-done.4, bf16[8,64,1536]{2,1,0:T(8,128)(2,1)S(1)} %copy-done.3, bf16[3,64,512]{2,1,0:T(8,128)(2,1)S(1)} %copy-done.6, ...), custom_call_target="tpu_custom_call", output_to_operand_aliasing={{}: (6, {})} | custom-call | flops 1 | bytes 1 | tf_op jit(solution)/shard_map/rest/pallas_call | solution.py:231
  (66 shorter events, 6.6 us)
Async XLA Ops:
  1.3 40.6 %collective-permute-start.1 = (bf16[8,64,4096]{2,1,0:T(8,128)(2,1)}, bf16[8,64,4096]{2,1,0:T(8,128)(2,1)}, u32[]{:S(2)}, u32[]{:S(2)}) collective-permute-start(bf16[8,64,4096]{2,1,0:T(8,128)(2,1)} %own_ref.5), channel_id=1, source_target_pairs={{0,1},{1,0},{2,3},{3,2},{4,5},{5,4},{6,7},{7,6},{8,9},{9,8},{10,11... | collective-permute-start | bytes 12582920 | tf_op jit(solution)/shard_map/ppermute | solution.py:263
  1.4 26.2 %collective-permute-start = (bf16[8,64,1024]{2,1,0:T(8,128)(2,1)S(1)}, bf16[8,64,1024]{2,1,0:T(8,128)(2,1)}, u32[]{:S(2)}, u32[]{:S(2)}) collective-permute-start(bf16[8,64,1024]{2,1,0:T(8,128)(2,1)S(1)} %slice.39), channel_id=1, source_target_pairs={{0,2},{2,0},{1,3},{3,1},{4,6},{6,4},{5,7},{7,5},{8,10},{10,8},{9,1... | collective-permute-start | bytes 3145736 | tf_op jit(solution)/shard_map/ppermute | solution.py:256
  3.1 15.2 %copy-start.14 = (bf16[32,32]{1,0:T(8,128)(2,1)S(1)}, bf16[32,32]{1,0:T(8,128)(2,1)}, u32[]{:S(2)}) copy-start(bf16[32,32]{1,0:T(8,128)(2,1)} %param.16) | copy-start | bytes 6148
  9.7 15.0 %all-to-all-start = ((bf16[8,64,512]{2,1,0:T(8,128)(2,1)}), bf16[8,64,512]{2,1,0:T(8,128)(2,1)S(1)}, u32[]{:S(2)}, u32[]{:S(2)}) async-start(bf16[8,64,512]{2,1,0:T(8,128)(2,1)} %bitcast.11), calls=%async_computation | async-start | bytes 1048576 | tf_op jit(solution)/shard_map/swap_rows/all_to_all | solution.py:279
  15.5 24.6 %copy-start.10 = (bf16[128,512]{1,0:T(8,128)(2,1)S(1)}, bf16[128,512]{1,0:T(8,128)(2,1)}, u32[]{:S(2)}) copy-start(bf16[128,512]{1,0:T(8,128)(2,1)} %constant.122.clone) | copy-start | bytes 393220
  15.5 24.6 %copy-start.11 = (bf16[128,8]{1,0:T(8,128)(2,1)S(1)}, bf16[128,8]{1,0:T(8,128)(2,1)}, u32[]{:S(2)}) copy-start(bf16[128,8]{1,0:T(8,128)(2,1)} %constant.120.clone) | copy-start | bytes 6148
  15.5 24.6 %copy-start.13 = (bf16[32,512]{1,0:T(8,128)(2,1)S(1)}, bf16[32,512]{1,0:T(8,128)(2,1)}, u32[]{:S(2)}) copy-start(bf16[32,512]{1,0:T(8,128)(2,1)} %constant.121.clone) | copy-start | bytes 98308
  15.5 25.1 %copy-start.16 = (f32[8]{0:T(128)S(1)}, f32[8]{0:T(128)}, u32[]{:S(2)}) copy-start(f32[8]{0:T(128)} %param.17) | copy-start | bytes 100
  15.5 25.3 %copy-start.12 = (bf16[128,256]{1,0:T(8,128)(2,1)S(1)}, bf16[128,256]{1,0:T(8,128)(2,1)}, u32[]{:S(2)}) copy-start(bf16[128,256]{1,0:T(8,128)(2,1)} %constant.124.clone) | copy-start | bytes 196612
  15.5 25.3 %copy-start.15 = (bf16[16,256]{1,0:T(8,128)(2,1)S(1)}, bf16[16,256]{1,0:T(8,128)(2,1)}, u32[]{:S(2)}) copy-start(bf16[16,256]{1,0:T(8,128)(2,1)} %constant.123.clone) | copy-start | bytes 24580
  17.9 41.2 %collective-permute-start.2 = (bf16[8,64,1024]{2,1,0:T(8,128)(2,1)}, bf16[8,64,1024]{2,1,0:T(8,128)(2,1)}, u32[]{:S(2)}, u32[]{:S(2)}) collective-permute-start(bf16[8,64,1024]{2,1,0:T(8,128)(2,1)} %slice.45), channel_id=1, source_target_pairs={{0,2},{2,0},{1,3},{3,1},{4,6},{6,4},{5,7},{7,5},{8,10},{10,8},{9,1... | collective-permute-start | bytes 3145736 | tf_op jit(solution)/shard_map/ppermute | solution.py:256
  28.9 22.8 %all-to-all-start.1 = ((bf16[32,8,512]{2,1,0:T(8,128)(2,1)}), bf16[32,8,512]{2,1,0:T(8,128)(2,1)S(1)}, u32[]{:S(2)}, u32[]{:S(2)}) async-start(bf16[32,8,512]{2,1,0:T(8,128)(2,1)} %fusion.10), calls=%async_computation.1 | async-start | bytes 524288 | tf_op jit(solution)/shard_map/swap_modes/all_to_all | solution.py:291
  40.6 7.4 %copy-start.7 = (bf16[128,512]{1,0:T(8,128)(2,1)}, bf16[128,512]{1,0:T(8,128)(2,1)S(1)}, u32[]{:S(2)}) copy-start(bf16[128,512]{1,0:T(8,128)(2,1)S(1)} %convolution_multiply_fusion.2.kron_ref) | copy-start | bytes 393220
  41.9 23.5 %copy-start.9 = (bf16[2,4,32,8,256]{4,3,2,1,0:T(8,128)(2,1)S(1)}, bf16[2,4,32,8,256]{4,3,2,1,0:T(8,128)(2,1)}, u32[]{:S(2)}) copy-start(bf16[2,4,32,8,256]{4,3,2,1,0:T(8,128)(2,1)} %param.15) | copy-start | bytes 3145732
  52.6 12.5 %all-to-all-start.2 = ((bf16[64,4,512]{2,1,0:T(4,128)(2,1)}), bf16[64,4,512]{2,1,0:T(4,128)(2,1)S(1)}, u32[]{:S(2)}, u32[]{:S(2)}) async-start(bf16[64,4,512]{2,1,0:T(4,128)(2,1)} %bitcast.17), calls=%async_computation.2 | async-start | bytes 524288 | tf_op jit(solution)/shard_map/gather_chan/all_to_all | solution.py:303
  57.0 10.2 %collective-permute-start.3 = (bf16[3,64,512]{2,1,0:T(8,128)(2,1)}, bf16[3,64,512]{2,1,0:T(8,128)(2,1)S(1)}, u32[]{:S(2)}, u32[]{:S(2)}) collective-permute-start(bf16[3,64,512]{2,1,0:T(8,128)(2,1)} %get-tuple-element.46), channel_id=1, source_target_pairs={{0,2},{2,0},{1,3},{3,1},{4,6},{6,4},{5,7},{7,5},{8,10},{10,8},{9,1... | collective-permute-start | bytes 589832 | tf_op jit(solution)/shard_map/ppermute | solution.py:256
  65.3 16.5 %collective-permute-start.5 = (bf16[8,64,1024]{2,1,0:T(8,128)(2,1)}, bf16[8,64,1024]{2,1,0:T(8,128)(2,1)S(1)}, u32[]{:S(2)}, u32[]{:S(2)}) collective-permute-start(bf16[8,64,1024]{2,1,0:T(8,128)(2,1)} %collective-permute-done.cross_ref), channel_id=1, source_target_pairs={{0,1},{1,0},{2,3},{3,2},{4,5},{5,4},{6,7},{7,6},{8,9},{9,8},{10,11... | collective-permute-start | bytes 3145736 | tf_op jit(solution)/shard_map/pointwise/ppermute | solution.py:146
  67.3 19.1 %copy-start.5 = (bf16[3,64,512]{2,1,0:T(8,128)(2,1)}, bf16[3,64,512]{2,1,0:T(8,128)(2,1)S(1)}, u32[]{:S(2)}) copy-start(bf16[3,64,512]{2,1,0:T(8,128)(2,1)S(1)} %collective-permute-done.3.half_ref) | copy-start | bytes 589828
  67.3 5.4 %collective-permute-start.4 = (bf16[8,4,512]{2,1,0:T(4,128)(2,1)S(1)}, bf16[8,4,512]{2,1,0:T(4,128)(2,1)S(1)}, u32[]{:S(2)}, u32[]{:S(2)}) collective-permute-start(bf16[8,4,512]{2,1,0:T(4,128)(2,1)S(1)} %pad_maximum_fusion.2), channel_id=1, source_target_pairs={{0,32},{32,0},{1,33},{33,1},{2,34},{34,2},{3,35},{35,3},{4,36},{36... | collective-permute-start | bytes 98312 | tf_op jit(solution)/shard_map/join_halves/ppermute | solution.py:320
  72.7 18.5 %collective-permute-start.6 = (bf16[8,64,512]{2,1,0:T(8,128)(2,1)}, bf16[8,64,512]{2,1,0:T(8,128)(2,1)}, u32[]{:S(2)}, u32[]{:S(2)}) collective-permute-start(bf16[8,64,512]{2,1,0:T(8,128)(2,1)} %get-tuple-element.53), channel_id=1, source_target_pairs={{0,2},{2,0},{1,3},{3,1},{4,6},{6,4},{5,7},{7,5},{8,10},{10,8},{9,1... | collective-permute-start | bytes 1572872 | tf_op jit(solution)/shard_map/join_halves/ppermute | solution.py:256
  73.9 17.3 %all-to-all-start.3 = ((bf16[32,8,512]{2,1,0:T(8,128)(2,1)}), bf16[32,8,512]{2,1,0:T(8,128)(2,1)S(1)}, u32[]{:S(2)}, u32[]{:S(2)}) async-start(bf16[32,8,512]{2,1,0:T(8,128)(2,1)} %bitcast.28), calls=%async_computation.3 | async-start | bytes 524288 | tf_op jit(solution)/shard_map/spread_modes/all_to_all | solution.py:330
  80.0 17.2 %collective-permute-start.8 = (bf16[8,64,1024]{2,1,0:T(8,128)(2,1)}, bf16[8,64,1024]{2,1,0:T(8,128)(2,1)}, u32[]{:S(2)}, u32[]{:S(2)}) collective-permute-start(bf16[8,64,1024]{2,1,0:T(8,128)(2,1)} %collective-permute-done.2.cross_ref), channel_id=1, source_target_pairs={{0,1},{1,0},{2,3},{3,2},{4,5},{5,4},{6,7},{7,6},{8,9},{9,8},{10,11... | collective-permute-start | bytes 3145736 | tf_op jit(solution)/shard_map/pointwise/ppermute | solution.py:146
  80.1 34.6 %collective-permute-start.7 = (bf16[21,64,512]{2,1,0:T(8,128)(2,1)}, bf16[21,64,512]{2,1,0:T(8,128)(2,1)S(1)}, u32[]{:S(2)}, u32[]{:S(2)}) collective-permute-start(bf16[21,64,512]{2,1,0:T(8,128)(2,1)} %get-tuple-element.58), channel_id=1, source_target_pairs={{0,2},{2,0},{1,3},{3,1},{4,6},{6,4},{5,7},{7,5},{8,10},{10,8},{9,1... | collective-permute-start | bytes 4128776 | tf_op jit(solution)/shard_map/join_halves/ppermute | solution.py:256
  81.9 1.0 copy-start.8
  92.4 11.6 %all-to-all-start.4 = ((bf16[8,64,512]{2,1,0:T(8,128)(2,1)}), bf16[8,64,512]{2,1,0:T(8,128)(2,1)S(1)}, u32[]{:S(2)}, u32[]{:S(2)}) async-start(bf16[8,64,512]{2,1,0:T(8,128)(2,1)} %bitcast.30), calls=%async_computation.4 | async-start | bytes 1048576 | tf_op jit(solution)/shard_map/swap_back/all_to_all | solution.py:341
  100.9 13.8 %copy-start.2 = (bf16[512,1536]{1,0:T(8,128)(2,1)S(1)}, bf16[512,1536]{1,0:T(8,128)(2,1)}, u32[]{:S(2)}) copy-start(bf16[512,1536]{1,0:T(8,128)(2,1)} %constant.125.clone.back_ref) | copy-start | bytes 4718596
  100.9 13.8 %copy-start.4 = (f32[128,1]{1,0:T(8,128)S(1)}, f32[128,1]{1,0:T(8,128)}, u32[]{:S(2)}) copy-start(f32[128,1]{1,0:T(8,128)} %copy.33.bias_ref) | copy-start | bytes 1540
  104.0 0.8 copy-start
  104.8 10.0 %copy-start.3 = (bf16[8,64,1536]{2,1,0:T(8,128)(2,1)S(1)}, bf16[8,64,1536]{2,1,0:T(8,128)(2,1)}, u32[]{:S(2)}) copy-start(bf16[8,64,1536]{2,1,0:T(8,128)(2,1)} %get-tuple-element.56.late_ref) | copy-start | bytes 4718596
  104.8 10.0 %copy-start.6 = (bf16[3,64,512]{2,1,0:T(8,128)(2,1)S(1)}, bf16[3,64,512]{2,1,0:T(8,128)(2,1)}, u32[]{:S(2)}) copy-start(bf16[3,64,512]{2,1,0:T(8,128)(2,1)} %copy-done.5) | copy-start | bytes 589828
  114.7 1.0 copy-start.1
